TPU v7x, 32 devices: a whole 2x2x4 slice. The times are simulated.
32 devices in a mesh: dp: 4 (over z), seq: 4 (over y, x), mp: 2 (over core).
Axes of the slice: x: 2, y: 2, z: 4, core: 2. Of those that a mesh axis runs over, the one named last changes fastest.
Arguments:
- inputs: bfloat16 [32, 2048, 1024], P('dp', ('seq', 'mp')), may hold values from -6 to 6
- gain_one: bfloat16 [1024], replicated, may hold values from 0.5 to 1.5
- w_query: bfloat16 [1024, 1024], P(None, 'mp'), may hold values from -0.1875 to 0.1875
- w_tied: bfloat16 [1024, 256], P(None, 'mp'), may hold values from -0.1875 to 0.1875
- w_rope: bfloat16 [1024, 32], replicated, may hold values from -0.1875 to 0.1875
- w_out: bfloat16 [1024, 1024], P('mp'), may hold values from -2 to 2
- gain_two: bfloat16 [1024], replicated, may hold values from 0.5 to 1.5
- w_gate: bfloat16 [1024, 2816], P(None, 'mp'), may hold values from -0.1875 to 0.1875
- w_up: bfloat16 [1024, 2816], P(None, 'mp'), may hold values from -0.1875 to 0.1875
- w_down: bfloat16 [2816, 1024], P('mp'), may hold values from -0.109375 to 0.109375
- doc_starts: int32 [32, 8], P('dp'), may hold values from 0 to 2048, as said below
- out_grad: bfloat16 [32, 2048, 1024], P('dp', ('seq', 'mp')), may hold values from -6 to 6
Outputs:
- outputs: bfloat16 [32, 2048, 1024], P('dp', ('seq', 'mp'))
- grad_inputs: float32 [32, 2048, 1024], P('dp', ('seq', 'mp'))
- grad_gain_one: float32 [1024], P(('dp', 'seq', 'mp'))
- grad_w_query: float32 [1024, 1024], P(('dp', 'seq'), 'mp')
- grad_w_tied: float32 [1024, 256], P(('dp', 'seq'), 'mp')
- grad_w_rope: float32 [1024, 32], P(('dp', 'seq', 'mp'))
- grad_w_out: float32 [1024, 1024], P('mp', ('dp', 'seq'))
- grad_gain_two: float32 [1024], P(('dp', 'seq', 'mp'))
- grad_w_gate: float32 [1024, 2816], P(('dp', 'seq'), 'mp')
- grad_w_up: float32 [1024, 2816], P(('dp', 'seq'), 'mp')
- grad_w_down: float32 [2816, 1024], P('mp', ('dp', 'seq'))
Inputs may be any that keep to these rules, and one draw needn't show every extreme that they name: `doc_starts`: row b lists where the documents of packed sequence b begin: the first entry is 0, entries never fall, and an entry equal to 2048 marks no document.
All inputs are finite; a program needn't handle non-finite values.
Results may differ from a plain program's by a relative error of at most 0.018.
Values may be sent and summed in bfloat16 or wider, within the bound.
A program may use at most 384 MiB of HBM per device.

v0:
```python
import functools

import jax
import jax.numpy as jnp
from jax import lax
from jax.experimental import pallas as pl
from jax.experimental.pallas import tpu as pltpu
from jax.sharding import PartitionSpec as P

HD = 64
RD = 32


epsilon = 1e-05
rope_base = 10000.0
masked_value = -1e30


def rope_tables(offset, count, rope_width):
    position = (offset + jnp.arange(count, dtype=jnp.int32)).astype(jnp.float32)
    frequency = rope_base ** (-jnp.arange(rope_width // 2, dtype=jnp.float32) * 2.0 / rope_width)
    angles = position[:, None] * frequency[None, :]
    return (jnp.cos(angles), jnp.sin(angles))


def rotate(values, cosine, sine_table):
    half_width = values.shape[-1] // 2
    first_half = values[..., :half_width]
    second_half = values[..., half_width:]
    return jnp.concatenate(
        [
            first_half * cosine - second_half * sine_table,
            second_half * cosine + first_half * sine_table,
        ],
        axis=-1,
    )


def rotate_back(grads, cosine, sine_table):
    half_width = grads.shape[-1] // 2
    first_half = grads[..., :half_width]
    second_half = grads[..., half_width:]
    return jnp.concatenate(
        [
            first_half * cosine + second_half * sine_table,
            second_half * cosine - first_half * sine_table,
        ],
        axis=-1,
    )


def contract_rows(left, right):
    return lax.dot_general(
        left, right, (((0,), (0,)), ((), ())), preferred_element_type=jnp.float32
    )


def times_transposed(left, right):
    return lax.dot_general(
        left, right, (((1,), (1,)), ((), ())), preferred_element_type=jnp.float32
    )


def norm_back(grad_normed, values, inverse, gain):
    scaled = grad_normed * gain
    grad_gain = jnp.sum(grad_normed * values * inverse, axis=(0, 1))
    grad_values = inverse * scaled - values * inverse**3 * jnp.mean(
        scaled * values, axis=-1, keepdims=True
    )
    return (grad_values, grad_gain)


def attend(operands):
    queries, key_full, values, allowed = operands
    scores = jnp.einsum(
        "qghd,kgd->ghqk", queries, key_full, preferred_element_type=jnp.float32
    ) * HD ** (-0.5)
    masked = jnp.where(allowed[None, None], scores, masked_value)
    row_max = jnp.max(masked, axis=-1, keepdims=True)
    weights = jnp.exp(masked - row_max)
    row_total = jnp.sum(weights, axis=-1, keepdims=True)
    attention_probs = (weights / row_total).astype(jnp.bfloat16)
    combined = jnp.einsum(
        "ghqk,kgd->qghd", attention_probs, values, preferred_element_type=jnp.float32
    )
    return (combined.astype(jnp.bfloat16), row_max + jnp.log(row_total))


def attend_back(operands):
    queries, key_full, values, allowed, log_total, grad_heads = operands
    score_scale = HD ** (-0.5)
    plain_width = HD - RD
    scores = (
        jnp.einsum("qghd,kgd->ghqk", queries, key_full, preferred_element_type=jnp.float32)
        * score_scale
    )
    masked = jnp.where(allowed[None, None], scores, masked_value)
    probs_float = jnp.exp(masked - log_total)
    grad_probs = jnp.einsum(
        "qghd,kgd->ghqk", grad_heads, values, preferred_element_type=jnp.float32
    )
    row_delta = jnp.sum(probs_float * grad_probs, axis=-1, keepdims=True)
    grad_scores = (probs_float * (grad_probs - row_delta)).astype(jnp.bfloat16)
    grad_queries = (
        jnp.einsum("ghqk,kgd->qghd", grad_scores, key_full, preferred_element_type=jnp.float32)
        * score_scale
    )
    grad_keys = (
        jnp.einsum("ghqk,qghd->kgd", grad_scores, queries, preferred_element_type=jnp.float32)
        * score_scale
    )
    grad_values = jnp.einsum(
        "ghqk,qghd->kgd",
        probs_float.astype(jnp.bfloat16),
        grad_heads,
        preferred_element_type=jnp.float32,
    )
    grad_tied = grad_values + jnp.concatenate(
        [grad_keys[..., :plain_width], jnp.zeros_like(grad_keys[..., plain_width:])], axis=-1
    )
    grad_rope = jnp.sum(grad_keys[..., plain_width:], axis=1)
    return (grad_queries, grad_tied, grad_rope)


def on_device(
    inputs,
    gain_one,
    w_query,
    w_tied,
    w_rope,
    w_out,
    gain_two,
    w_gate,
    w_up,
    w_down,
    doc_starts,
    out_grad,
):
    seq_count, own_count, model_width = inputs.shape
    plain_width = HD - RD
    group_local = w_tied.shape[1] // HD
    head_local = w_query.shape[1] // HD
    seq_index = lax.axis_index("seq")
    mp_index = lax.axis_index("mp")
    gain_one_float = gain_one.astype(jnp.float32)
    gain_two_float = gain_two.astype(jnp.float32)
    inputs_float = inputs.astype(jnp.float32)
    inverse_one = lax.rsqrt(jnp.mean(inputs_float * inputs_float, axis=-1, keepdims=True) + epsilon)
    normed_one = (inputs_float * inverse_one * gain_one_float).astype(jnp.bfloat16)
    gathered_one = lax.all_gather(normed_one, "mp", axis=1, tiled=True)
    context = gathered_one.shape[1]
    token_count = seq_count * context
    flat_one = gathered_one.reshape(token_count, model_width)
    offset = seq_index * context
    cosine, sine_table = rope_tables(offset, context, RD)
    query_lin = jnp.dot(flat_one, w_query, preferred_element_type=jnp.float32).reshape(
        seq_count, context, head_local, HD
    )
    queries = jnp.concatenate(
        [
            query_lin[..., :plain_width],
            rotate(
                query_lin[..., plain_width:], cosine[None, :, None, :], sine_table[None, :, None, :]
            ),
        ],
        axis=-1,
    ).astype(jnp.bfloat16)
    queries = queries.reshape(seq_count, context, group_local, head_local // group_local, HD)
    tied_state = (
        jnp.dot(flat_one, w_tied, preferred_element_type=jnp.float32)
        .astype(jnp.bfloat16)
        .reshape(seq_count, context, group_local * HD)
    )
    rope_lin = jnp.dot(flat_one, w_rope, preferred_element_type=jnp.float32).reshape(
        seq_count, context, RD
    )
    rope_keys = rotate(rope_lin, cosine[None], sine_table[None]).astype(jnp.bfloat16)
    tied_all, rope_all = (
        lax.all_gather(tied_state, "seq", axis=1, tiled=True),
        lax.all_gather(rope_keys, "seq", axis=1, tiled=True),
    )
    length = tied_all.shape[1]
    values_all = tied_all.reshape(seq_count, length, group_local, HD)
    key_full = jnp.concatenate(
        [
            values_all[..., :plain_width],
            jnp.broadcast_to(rope_all[:, :, None, :], (seq_count, length, group_local, RD)),
        ],
        axis=-1,
    )
    key_position = jnp.arange(length, dtype=jnp.int32)
    key_segment = jnp.sum(
        (doc_starts[:, None, :] <= key_position[None, :, None]).astype(jnp.int32), axis=-1
    )
    query_segment = lax.dynamic_slice_in_dim(key_segment, offset, context, 1)
    query_position = offset + jnp.arange(context, dtype=jnp.int32)
    allowed = (query_segment[:, :, None] == key_segment[:, None, :]) & (
        query_position[:, None] >= key_position[None, :]
    )[None]
    head_outputs, log_total = lax.map(attend, (queries, key_full, values_all, allowed))
    flat_heads = head_outputs.reshape(token_count, head_local * HD)
    attended_part = jnp.dot(flat_heads, w_out, preferred_element_type=jnp.float32).reshape(
        seq_count, context, model_width
    )
    attended = lax.psum_scatter(
        attended_part.astype(jnp.bfloat16), "mp", scatter_dimension=1, tiled=True
    ).astype(jnp.float32)
    hidden = inputs_float + attended
    inverse_two = lax.rsqrt(jnp.mean(hidden * hidden, axis=-1, keepdims=True) + epsilon)
    normed_two = (hidden * inverse_two * gain_two_float).astype(jnp.bfloat16)
    gathered_two = lax.all_gather(normed_two, "mp", axis=1, tiled=True)
    flat_two = gathered_two.reshape(token_count, model_width)
    gate_values = jnp.dot(flat_two, w_gate, preferred_element_type=jnp.float32)
    up_values = jnp.dot(flat_two, w_up, preferred_element_type=jnp.float32)
    sigmoid_gate = jax.nn.sigmoid(gate_values)
    silu_gate = gate_values * sigmoid_gate
    active = (silu_gate * up_values).astype(jnp.bfloat16)
    result_part = jnp.dot(active, w_down, preferred_element_type=jnp.float32).reshape(
        seq_count, context, model_width
    )
    result = lax.psum_scatter(
        result_part.astype(jnp.bfloat16), "mp", scatter_dimension=1, tiled=True
    ).astype(jnp.float32)
    outputs = (hidden + result).astype(jnp.bfloat16)
    grad_out_all = lax.all_gather(out_grad, "mp", axis=1, tiled=True)
    flat_grad = grad_out_all.reshape(token_count, model_width)
    grad_active = times_transposed(flat_grad, w_down)
    grad_w_down = contract_rows(active, flat_grad)
    grad_gate = (
        grad_active * up_values * sigmoid_gate * (1.0 + gate_values * (1.0 - sigmoid_gate))
    ).astype(jnp.bfloat16)
    grad_up = (grad_active * silu_gate).astype(jnp.bfloat16)
    grad_w_gate = contract_rows(flat_two, grad_gate)
    grad_w_up = contract_rows(flat_two, grad_up)
    grad_two_part = (times_transposed(grad_gate, w_gate) + times_transposed(grad_up, w_up)).reshape(
        seq_count, context, model_width
    )
    grad_normed_two = lax.psum_scatter(
        grad_two_part.astype(jnp.bfloat16), "mp", scatter_dimension=1, tiled=True
    ).astype(jnp.float32)
    grad_hidden_norm, grad_gain_two = norm_back(
        grad_normed_two, hidden, inverse_two, gain_two_float
    )
    grad_hidden = out_grad.astype(jnp.float32) + grad_hidden_norm
    grad_attended_all = lax.all_gather(grad_hidden.astype(jnp.bfloat16), "mp", axis=1, tiled=True)
    flat_attended = grad_attended_all.reshape(token_count, model_width)
    grad_w_out = contract_rows(flat_heads, flat_attended)
    grad_heads = times_transposed(flat_attended, w_out).astype(jnp.bfloat16).reshape(queries.shape)
    grad_queries, grad_tied, grad_rope = lax.map(
        attend_back, (queries, key_full, values_all, allowed, log_total, grad_heads)
    )
    grad_queries = grad_queries.reshape(seq_count, context, head_local, HD)
    grad_query_lin = (
        jnp.concatenate(
            [
                grad_queries[..., :plain_width],
                rotate_back(
                    grad_queries[..., plain_width:],
                    cosine[None, :, None, :],
                    sine_table[None, :, None, :],
                ),
            ],
            axis=-1,
        )
        .astype(jnp.bfloat16)
        .reshape(token_count, head_local * HD)
    )
    tied_own, rope_context = (
        lax.psum_scatter(
            grad_tied.reshape(seq_count, length, group_local * HD).astype(jnp.bfloat16),
            "seq",
            scatter_dimension=1,
            tiled=True,
        ).astype(jnp.float32),
        lax.psum_scatter(
            grad_rope.astype(jnp.bfloat16), "seq", scatter_dimension=1, tiled=True
        ).astype(jnp.float32),
    )
    grad_tied_flat = tied_own.astype(jnp.bfloat16).reshape(token_count, group_local * HD)
    grad_one_part = (
        times_transposed(grad_query_lin, w_query) + times_transposed(grad_tied_flat, w_tied)
    ).reshape(seq_count, context, model_width)
    grad_normed_one, rope_own = (
        lax.psum_scatter(
            grad_one_part.astype(jnp.bfloat16), "mp", scatter_dimension=1, tiled=True
        ).astype(jnp.float32),
        lax.psum_scatter(
            rope_context.astype(jnp.bfloat16), "mp", scatter_dimension=1, tiled=True
        ).astype(jnp.float32),
    )
    own_offset = offset + mp_index * own_count
    cosine_own, sine_own = rope_tables(own_offset, own_count, RD)
    grad_rope_flat = (
        rotate_back(rope_own, cosine_own[None], sine_own[None])
        .astype(jnp.bfloat16)
        .reshape(seq_count * own_count, RD)
    )
    grad_normed_one = grad_normed_one + times_transposed(grad_rope_flat, w_rope).reshape(
        seq_count, own_count, model_width
    )
    grad_w_rope = contract_rows(
        normed_one.reshape(seq_count * own_count, model_width), grad_rope_flat
    )
    grad_w_query = contract_rows(flat_one, grad_query_lin)
    grad_w_tied = contract_rows(flat_one, grad_tied_flat)
    grad_inputs_norm, grad_gain_one = norm_back(
        grad_normed_one, inputs_float, inverse_one, gain_one_float
    )
    grad_inputs = grad_hidden + grad_inputs_norm
    small_sums = (
        lax.psum_scatter(grad_gain_one, ("dp", "seq", "mp"), scatter_dimension=0, tiled=True),
        lax.psum_scatter(grad_w_rope, ("dp", "seq", "mp"), scatter_dimension=0, tiled=True),
        lax.psum_scatter(grad_gain_two, ("dp", "seq", "mp"), scatter_dimension=0, tiled=True),
    )
    weight_terms = (grad_w_query, grad_w_tied, grad_w_out, grad_w_gate, grad_w_up, grad_w_down)
    weight_sums = (
        lax.psum_scatter(weight_terms[0], ("dp", "seq"), scatter_dimension=0, tiled=True),
        lax.psum_scatter(weight_terms[1], ("dp", "seq"), scatter_dimension=0, tiled=True),
        lax.psum_scatter(weight_terms[2], ("dp", "seq"), scatter_dimension=1, tiled=True),
        lax.psum_scatter(weight_terms[3], ("dp", "seq"), scatter_dimension=0, tiled=True),
        lax.psum_scatter(weight_terms[4], ("dp", "seq"), scatter_dimension=0, tiled=True),
        lax.psum_scatter(weight_terms[5], ("dp", "seq"), scatter_dimension=1, tiled=True),
    )
    return (
        outputs,
        grad_inputs,
        small_sums[0],
        weight_sums[0],
        weight_sums[1],
        small_sums[1],
        weight_sums[2],
        small_sums[2],
        weight_sums[3],
        weight_sums[4],
        weight_sums[5],
    )


BF = jnp.bfloat16
F32 = jnp.float32
NN = (((1,), (0,)), ((), ()))
NT = (((1,), (1,)), ((), ()))
TN = (((0,), (0,)), ((), ()))
BIG = 2.0**100
MIB = 1 << 20
LANE = 128


def mxu(left, right, dims):
    return lax.dot_general(left, right, dims, preferred_element_type=F32)


def params(limit=56):
    return pltpu.CompilerParams(vmem_limit_bytes=limit * MIB)


def cost(flops, moved=0):
    return pl.CostEstimate(flops=int(flops), bytes_accessed=int(moved), transcendentals=0)


def swap_cores(value):
    return lax.ppermute(value, "mp", [(0, 1), (1, 0)])


def shift(value, axis, by):
    size = lax.axis_size(axis)
    return lax.ppermute(value, axis, [(i, (i + by) % size) for i in range(size)])


def send_near(kv):
    return [kv] + [shift(kv, "seq", k) for k in range(1, lax.axis_size("seq"))]


def send_far(near):
    return [part[None] for part in near + [swap_cores(value) for value in near]]


def pick(value, index, axis):
    return lax.dynamic_index_in_dim(value, index, axis, keepdims=False)


def send_steps(value, axis, dim):
    size, me = lax.axis_size(axis), lax.axis_index(axis)
    terms = [pick(value, me, dim)]
    for k in range(1, size):
        terms.append(shift(pick(value, (me + k) % size, dim), axis, k))
    return terms


def add_up(terms):
    total = terms[0].astype(F32)
    for term in terms[1:]:
        total = total + term.astype(F32)
    return total


def by_core(own, other, axis):
    first = lax.axis_index("mp") == 0
    return jnp.concatenate(
        [jnp.where(first, own, other), jnp.where(first, other, own)], axis=axis
    )


def rotate_rows(values, cosine, sine_table):
    half = values.shape[0] // 2
    a, b = values[:half], values[half:]
    return jnp.concatenate([a * cosine - b * sine_table, b * cosine + a * sine_table], axis=0)


def project_kernel(
    sent, x_ref, og_ref, gain_ref, wqo_ref, wqp_ref, wto_ref, wtp_ref, wr_ref, wdo_ref, wdp_ref,
    cos_ref, sin_ref, kv_ref, nt_ref, q_ref, ga_ref, wq_ref, wkv_ref, near_ref, far_ref,
    kept, wd, load_sems, own_sems, sends, receives,
):
    b = pl.program_id(0)
    count_s = lax.axis_size("seq")
    me_s, core = lax.axis_index("seq"), lax.axis_index("mp")
    peers = [{"seq": lax.rem(me_s + k, count_s)} for k in range(1, count_s)]
    other_core = {"mp": 1 - core}
    near, forward = [], []
    slots = iter(range(sends.shape[0]))

    def link(source, target, peer):
        slot = next(slots)
        return pltpu.make_async_remote_copy(
            src_ref=source,
            dst_ref=target,
            send_sem=sends.at[slot],
            recv_sem=receives.at[slot],
            device_id=peer,
            device_id_type=pl.DeviceIdType.MESH,
        )

    for i in range(sent):
        near.append([link(kept.at[i], near_ref.at[k, i], peers[k - 1]) for k in range(1, count_s)])
        forward.append(
            [link(kept.at[i], far_ref.at[0, i], other_core)]
            + [link(near_ref.at[k, i], far_ref.at[k, i], other_core) for k in range(1, count_s)]
        )
    own = [pltpu.make_async_copy(kept.at[i], near_ref.at[0, i], own_sems.at[i]) for i in range(sent)]
    loads = load_weights([(wdo_ref, 0, 0), (wdp_ref, 1, 0)], [wd, wd], load_sems)

    @pl.when(b == 0)
    def _():
        for copy in loads:
            copy.start()
        barrier = pltpu.get_barrier_semaphore()
        for peer in [other_core] + peers:
            pl.semaphore_signal(barrier, inc=1, device_id=peer, device_id_type=pl.DeviceIdType.MESH)
        pl.semaphore_wait(barrier, count_s)

        def turn(source, target, at):
            size = source.shape[1]
            row = lax.broadcasted_iota(jnp.int32, (size, size), 0)
            column = lax.broadcasted_iota(jnp.int32, (size, size), 1)
            identity = jnp.where(row == column, 1.0, 0.0).astype(BF)
            target[pl.ds(at, size)] = mxu(identity, source[...], NT).astype(BF)

        for pair, target in (((wto_ref, wtp_ref), wkv_ref), ((wqo_ref, wqp_ref), wq_ref)):
            size = pair[0].shape[1]
            for side, source in enumerate(pair):
                place = jnp.where(core == side, 0, 1)
                turn(source, target, pl.multiple_of(place * size, size))
        turn(wr_ref, wkv_ref, wkv_ref.shape[0] - RD)
        for copy in loads:
            copy.wait()

    x = x_ref[0].astype(F32)
    inverse = lax.rsqrt(jnp.mean(x * x, axis=-1, keepdims=True) + epsilon)
    normed = (x * inverse * gain_ref[...]).astype(BF)
    lin = mxu(wkv_ref[...], normed, NT)
    tied = wkv_ref.shape[0] - RD
    cosine, sine_table = cos_ref[...], sin_ref[...]
    rope = rotate_rows(lin[tied:], cosine, sine_table)
    keys = jnp.concatenate([lin[:tied], rope], axis=0).astype(BF)
    @pl.when(b >= sent)
    def _():
        kv_ref[0] = keys

    for i in range(sent):

        @pl.when(b == i)
        def _():
            kept[i] = keys
            for copy in near[i]:
                copy.start()
            forward[i][0].start()
            own[i].start()

    nt_ref[0] = normed.T
    lin = mxu(wq_ref[...], normed, NT)
    plain = HD - RD
    pieces = []
    for at in range(0, lin.shape[0], HD):
        pieces.append(lin[at : at + plain])
        pieces.append(rotate_rows(lin[at + plain : at + HD], cosine, sine_table))
    queries = jnp.concatenate(pieces, axis=0)
    q_ref[0] = (queries.astype(BF) * HD ** (-0.5)).astype(BF)

    og = og_ref[0]
    for at in range(0, wd.shape[0], 2 * LANE):
        to = slice(at, at + 2 * LANE)
        ga_ref[:, to] = mxu(og, wd[to], NT).astype(BF)

    steps = pl.num_programs(0)
    for i in range(sent):

        @pl.when(b == steps - sent + i)
        def _():
            for copy in near[i]:
                copy.wait()
            for copy in forward[i][1:]:
                copy.start()

    @pl.when(b == steps - 1)
    def _():
        for i in range(sent):
            own[i].wait()
            for copy in forward[i]:
                copy.wait()


def project(x, og, gain, wq, wt, wr, wd, cosine, sine_table, sent):
    count, own, width = x.shape
    rows, half = 2 * wq[0].shape[1], wd[0].shape[0]
    kv_rows = 2 * wt[0].shape[1] + wr.shape[1]
    weights = [*wq, *wt, wr]
    count_s = lax.axis_size("seq")
    whole = lambda array: pl.BlockSpec(array.shape, lambda b: (0, 0))
    seq = pl.BlockSpec((1, own, width), lambda b: (b, 0, 0))
    hbm = pl.BlockSpec(memory_space=pl.ANY)
    gathered = jax.ShapeDtypeStruct((count_s, sent, kv_rows, own), BF)
    links = sent * (2 * count_s - 1)
    return pl.pallas_call(
        functools.partial(project_kernel, sent),
        grid=(count,),
        in_specs=[
            seq, seq, whole(gain), *[whole(part) for part in weights], hbm, hbm, whole(cosine),
            whole(cosine),
        ],
        out_specs=[
            pl.BlockSpec((1, kv_rows, own), lambda b: (jnp.maximum(b - sent, 0), 0, 0)),
            pl.BlockSpec((1, width, own), lambda b: (b, 0, 0)),
            pl.BlockSpec((1, rows, own), lambda b: (b, 0, 0)),
            pl.BlockSpec((own, 2 * half), lambda b: (b, 0)),
            pl.BlockSpec((rows, width), lambda b: (0, 0)),
            pl.BlockSpec((kv_rows, width), lambda b: (0, 0)),
            hbm,
            hbm,
        ],
        out_shape=[
            jax.ShapeDtypeStruct((count - sent, kv_rows, own), BF),
            jax.ShapeDtypeStruct((count, width, own), BF),
            jax.ShapeDtypeStruct((count, rows, own), BF),
            jax.ShapeDtypeStruct((count * own, 2 * half), BF),
            jax.ShapeDtypeStruct((rows, width), BF),
            jax.ShapeDtypeStruct((kv_rows, width), BF),
            gathered,
            gathered,
        ],
        scratch_shapes=[
            pltpu.VMEM((sent, kv_rows, own), BF),
            pltpu.VMEM((2 * half, width), BF),
            pltpu.SemaphoreType.DMA((2 * (half // LANE),)),
            pltpu.SemaphoreType.DMA((sent,)),
            pltpu.SemaphoreType.DMA((links,)),
            pltpu.SemaphoreType.DMA((links,)),
        ],
        compiler_params=pltpu.CompilerParams(
            vmem_limit_bytes=56 * MIB, collective_id=2, has_side_effects=True
        ),
        cost_estimate=cost(3 * 10**10),
        name="project",
    )(x, og, gain, *weights, *wd, cosine, sine_table)


def segment_counts(starts, first, width):
    position = first + lax.broadcasted_iota(jnp.int32, (1, width), 1)
    count = jnp.zeros((1, width), jnp.int32)
    for start in starts:
        count = count + (start <= position).astype(jnp.int32)
    return count


def query_rows(starts, first, width):
    row = lax.broadcasted_iota(jnp.int32, (16, width), 0)
    match = segment_counts(starts, first, width) == row + 1
    return jnp.where(match, 1.0, 0.0).astype(BF)


def key_rows(starts, first, width):
    row = lax.broadcasted_iota(jnp.int32, (16, width), 0)
    match = (segment_counts(starts, first, width) == row + 1) | (row >= len(starts))
    return jnp.where(match, 0.0, -BIG).astype(BF)


def first_rows(count, width):
    row = lax.broadcasted_iota(jnp.int32, (16, width), 0)
    return jnp.where(row < count, 1.0, 0.0).astype(BF)


def three_parts(row, width):
    high = row.astype(BF)
    rest = row - high.astype(F32)
    middle = rest.astype(BF)
    low = (rest - middle.astype(F32)).astype(BF)
    at = lax.broadcasted_iota(jnp.int32, (16, width), 0)
    parts = jnp.where(at == 0, high.astype(F32), 0.0)
    parts = jnp.where(at == 1, middle.astype(F32), parts)
    return jnp.where(at == 2, low.astype(F32), parts).astype(BF)


def start_chunk(starts, first, chunk):
    begin = jnp.int32(0)
    for start in starts:
        begin = jnp.where(start <= first, jnp.maximum(begin, start), begin)
    return begin // chunk


def my_chunk():
    return lax.axis_index("seq") * lax.axis_size("mp") + lax.axis_index("mp")


def place_keys(refs, kv, begin, me):
    steps = lax.axis_size("seq")
    seq, core = lax.axis_index("seq"), lax.axis_index("mp")
    places = [(ref, i) for ref in refs for i in range(ref.shape[0])]
    for at, (ref, i) in enumerate(places):
        of = core if at < steps else 1 - core
        j = lax.rem(seq - at % steps + steps, steps) * 2 + of

        @pl.when((j >= begin) & (j <= me))
        def _():
            kv[j] = ref[i, 0]


def stack_heads(value, at, heads, rows=HD):
    half = value.shape[1] // 2
    return jnp.concatenate(
        [
            value[at + h * rows : at + (h + 1) * rows, s * half : (s + 1) * half]
            for s in range(2)
            for h in range(heads)
        ],
        axis=1,
    )


def stack_queries(starts, first, half, heads):
    return jnp.concatenate(
        [query_rows(starts, first + s * half, half) for s in range(2) for _ in range(heads)], axis=1
    )


def attend_kernel(groups, heads, first, inputs, docs_ref, q_ref, *refs):
    kv_refs = refs[:inputs]
    out_ref, lse_ref, kv_ref, qa, acc, top = refs[-6:]
    b = pl.program_id(0) + first
    own = q_ref.shape[2]
    ndoc = docs_ref.shape[1]
    starts = [docs_ref[b, k] for k in range(ndoc)]
    me = my_chunk()
    begin = start_chunk(starts, me * own, own)
    half = own // 2
    begin_second = start_chunk(starts, me * own + half, own)
    place_keys(kv_refs, kv_ref, begin, me)
    wide = heads * own
    first_half = wide // 2
    tied = groups * HD
    plain = HD - RD
    q_doc = stack_queries(starts, me * own, half, heads)
    q_all = q_ref[0]
    for g in range(groups):
        qa[g, :HD] = stack_heads(q_all, g * heads * HD, heads)
        qa[g, HD : HD + 16] = q_doc
        qa[g, HD + 16 :] = jnp.zeros((LANE - HD - 16, wide), BF)
    ones = first_rows(1, own)
    zeros = jnp.zeros((LANE - HD - 16, own), BF)

    def keys_of(j, g):
        doc = key_rows(starts, j * own, own)
        block = jnp.concatenate(
            [
                kv_ref[j, g * HD : g * HD + plain],
                kv_ref[j, tied : tied + RD],
                doc,
                zeros,
            ],
            axis=0,
        )
        return block.T

    def values_of(j, g):
        return jnp.concatenate([kv_ref[j, g * HD : (g + 1) * HD], ones], axis=0)

    key_at = lax.broadcasted_iota(jnp.int32, (own, half), 0)
    query_at = lax.broadcasted_iota(jnp.int32, (own, half), 1)
    causal = jnp.concatenate(
        [key_at <= query_at + s * half for s in range(2) for _ in range(heads)], axis=1
    )

    def block(j, lanes, diagonal=False):
        def logits_of(g):
            return mxu(keys_of(j, g), qa[g, :, lanes], NN)

        following = logits_of(0)
        for g in range(groups):
            logits = following
            if g + 1 < groups:
                following = logits_of(g + 1)
            if diagonal:
                logits = jnp.where(causal, logits, masked_value)
            peak = jnp.max(logits, axis=0, keepdims=True)
            if not diagonal:
                old = top[g, :, lanes]
                peak = jnp.maximum(old, peak)
            weights = jnp.exp(logits - peak).astype(BF)
            added = mxu(values_of(j, g), weights, NN)
            if not diagonal:
                added = acc[g, :, lanes] * jnp.exp(old - peak) + added
            acc[g, :, lanes] = added
            top[g, :, lanes] = peak

    block(me, slice(0, wide), True)

    def both(i, carry):
        block(me - 1 - i, slice(0, wide))
        return carry

    def first_only(i, carry):
        block(begin_second - 1 - i, slice(0, first_half))
        return carry

    lax.fori_loop(0, me - begin_second, both, 0)
    lax.fori_loop(0, begin_second - begin, first_only, 0)
    for g in range(groups):
        total = acc[g, HD : HD + 1]
        result = acc[g, :HD] / total
        lse_ref[0, g : g + 1] = top[g] + jnp.log(total)
        for s in range(2):
            for h in range(heads):
                at, of = (g * heads + h) * HD, (s * heads + h) * half
                out_ref[0, at : at + HD, s * half : (s + 1) * half] = result[:, of : of + half].astype(BF)


def kv_specs(kv, kv_at):
    return [
        pl.BlockSpec((part.shape[0], 1, *part.shape[2:]), lambda b: (0, b + kv_at, 0, 0))
        for part in kv
    ]


def attend_forward(docs, q, kv, groups, heads, first, size, kv_at, into):
    kv_rows, own = kv[0].shape[2:]
    count, chunks, inputs = docs.shape[0], 2 * lax.axis_size("seq"), len(kv)
    wide = heads * own
    hbm = pl.BlockSpec(memory_space=pl.ANY)
    return pl.pallas_call(
        functools.partial(attend_kernel, groups, heads, first, inputs),
        grid=(size,),
        in_specs=[
            pl.BlockSpec(memory_space=pltpu.SMEM),
            pl.BlockSpec((1, q.shape[1], own), lambda b: (b + first, 0, 0)),
        ]
        + kv_specs(kv, kv_at)
        + [hbm] * len(into),
        out_specs=[
            pl.BlockSpec((1, q.shape[1], own), lambda b: (b + first, 0, 0)),
            pl.BlockSpec((1, groups, wide), lambda b: (b + first, 0, 0)),
        ],
        out_shape=[
            jax.ShapeDtypeStruct(q.shape, BF),
            jax.ShapeDtypeStruct((count, groups, wide), F32),
        ],
        scratch_shapes=[
            pltpu.VMEM((chunks, kv_rows, own), BF),
            pltpu.VMEM((groups, LANE, wide), BF),
            pltpu.VMEM((groups, HD + 16, wide), F32),
            pltpu.VMEM((groups, 1, wide), F32),
        ],
        input_output_aliases={2 + inputs + i: i for i in range(len(into))},
        compiler_params=params(),
        cost_estimate=cost(10**10 * size),
        name="attend",
    )(docs, q, *kv, *into)


def attend_back_kernel(
    groups, heads, first, inputs, docs_ref, q_ref, do_ref, lse_ref, delta_ref, rot_ref, *refs
):
    kv_refs = refs[:inputs]
    chunks = 2 * lax.axis_size("seq")
    dq_ref, keep_ref, give_ref, kv_ref, stage, qs, qa, ds_, da, dq = refs[-10:]
    b = pl.program_id(0) + first
    own = q_ref.shape[2]
    ndoc = docs_ref.shape[1]
    starts = [docs_ref[b, k] for k in range(ndoc)]
    me = my_chunk()
    begin = start_chunk(starts, me * own, own)
    half = own // 2
    begin_second = start_chunk(starts, me * own + half, own)
    place_keys(kv_refs, kv_ref, begin, me)
    wide = heads * own
    tied = groups * HD
    plain = HD - RD
    q_doc = stack_queries(starts, me * own, half, heads)
    q_all, do_all = q_ref[0], do_ref[0]
    pad_q = jnp.zeros((LANE - HD - 32, wide), BF)
    pad_d = jnp.zeros((LANE - HD - 16, wide), BF)
    row_at = lax.broadcasted_iota(jnp.int32, (own, own), 0)
    column_at = lax.broadcasted_iota(jnp.int32, (own, own), 1)
    identity = jnp.where(row_at == column_at, 1.0, 0.0).astype(BF)

    def turn(rows, ref):
        for h in range(0, heads, 2):
            pair = [rows[:, (h + i) * own : (h + i + 1) * own] for i in range(2)]
            turned = mxu(identity, jnp.concatenate(pair, axis=0), NT).astype(BF)
            ref[h * own : (h + 1) * own] = turned[:, :LANE]
            ref[(h + 1) * own : (h + 2) * own] = turned[:, LANE:]

    for g in range(groups):
        q_rows = stack_heads(q_all, g * heads * HD, heads)
        do_rows = stack_heads(do_all, g * heads * HD, heads)
        qs[g] = q_rows
        ds_[g] = do_rows
        lse_rows = three_parts(-lse_ref[0, g : g + 1], wide)
        delta_row = stack_heads(delta_ref[0], g * heads, heads, 1)
        delta_rows = three_parts(-delta_row, wide)
        turn(jnp.concatenate([q_rows, q_doc, lse_rows, pad_q], axis=0), qa.at[g])
        turn(jnp.concatenate([do_rows, delta_rows, pad_d], axis=0), da.at[g])
    ones = first_rows(3, own)
    pad_k = jnp.zeros((LANE - HD - 32, own), BF)
    pad_v = jnp.zeros((LANE - HD - 16, own), BF)

    seq, core = lax.axis_index("seq"), lax.axis_index("mp")
    steps = chunks // 2

    def deliver(j, value):
        k = lax.rem(j // 2 - seq + steps, steps)

        @pl.when(lax.rem(j, 2) == core)
        def _():
            keep_ref[k, 0] = value()

        @pl.when(lax.rem(j, 2) != core)
        def _():
            give_ref[k, 0] = value()

    def clear(j, carry):
        deliver(j, lambda: jnp.zeros(keep_ref.shape[2:], BF))
        return carry

    lax.fori_loop(0, begin, clear, 0)
    lax.fori_loop(me + 1, chunks, clear, 0)

    def block(j, rows, diagonal):
        doc = key_rows(starts, j * own, own)
        rope_rows = kv_ref[j, tied : tied + RD]
        rope_sum = jnp.zeros((RD, own), F32)

        def keys_of(g):
            return jnp.concatenate(
                [kv_ref[j, g * HD : g * HD + plain], rope_rows], axis=0
            )

        def products(g):
            values = kv_ref[j, g * HD : (g + 1) * HD]
            return (
                mxu(qa[g, :rows], jnp.concatenate([keys_of(g), doc, ones, pad_k], axis=0), NN),
                mxu(da[g, :rows], jnp.concatenate([values, ones, pad_v], axis=0), NN),
            )

        following = products(0)
        for g in range(groups):
            logits, slopes = following
            if g + 1 < groups:
                following = products(g + 1)
            keys = keys_of(g)
            weights = jnp.exp(logits)
            if diagonal:
                query_at = lax.broadcasted_iota(jnp.int32, (half, own), 0)
                key_at = lax.broadcasted_iota(jnp.int32, (half, own), 1)
                causal = jnp.concatenate(
                    [key_at <= query_at + s * half for s in range(2) for _ in range(heads)], axis=0
                )
                weights = jnp.where(causal, weights, 0.0)
            grads = (weights * slopes).astype(BF)
            grad_values = mxu(ds_[g, :, :rows], weights.astype(BF), NN)
            grad_keys = mxu(qs[g, :, :rows], grads, NN)
            keys_t = keys.T
            grad_queries = mxu(grads, jnp.concatenate([keys_t, keys_t], axis=1), NN)
            if diagonal:
                dq[g] = grad_queries
            else:
                dq[g, :rows] += grad_queries
            stage[g * HD : g * HD + plain] = (
                grad_values[:plain] + grad_keys[:plain]
            ).astype(BF)
            stage[g * HD + plain : (g + 1) * HD] = grad_values[plain:].astype(BF)
            rope_sum = rope_sum + grad_keys[plain:]
        stage[tied : tied + RD] = rope_sum.astype(BF)
        deliver(j, lambda: stage[...])

    block(me, wide, True)

    def both(j, carry):
        block(j, wide, False)
        return carry

    def first_only(j, carry):
        block(j, wide // 2, False)
        return carry

    lax.fori_loop(begin_second, me, both, 0)
    lax.fori_loop(begin, begin_second, first_only, 0)
    straight, ahead, behind = rot_ref[0], rot_ref[1], rot_ref[2]
    lane = lax.broadcasted_iota(jnp.int32, (half, LANE), 1)
    quarter = RD // 2
    for g in range(groups):
        for s in range(2):
            positions = slice(s * half, (s + 1) * half)
            for pair in range(heads // 2):
                at = (s * heads + 2 * pair) * half
                two = jnp.where(lane < HD, dq[g, at : at + half], dq[g, at + half : at + 2 * half])
                turned = (
                    two * straight[positions]
                    + pltpu.roll(two, LANE - quarter, 1) * ahead[positions]
                    + pltpu.roll(two, quarter, 1) * behind[positions]
                )
                to = (g * heads + 2 * pair) * HD
                dq_ref[positions, to : to + 2 * HD] = turned.astype(BF)


def attend_backward(docs, q, do, lse, delta, turns, kv, groups, heads, first, size, kv_at, into):
    kv_rows, own = kv[0].shape[2:]
    count, chunks, inputs = docs.shape[0], 2 * lax.axis_size("seq"), len(kv)
    wide = heads * own
    width = q.shape[1]
    column = pl.BlockSpec((1, width, own), lambda b: (b + first, 0, 0))
    hbm = pl.BlockSpec(memory_space=pl.ANY)
    return pl.pallas_call(
        functools.partial(attend_back_kernel, groups, heads, first, inputs),
        grid=(size,),
        in_specs=[
            pl.BlockSpec(memory_space=pltpu.SMEM),
            column,
            column,
            pl.BlockSpec((1, groups, wide), lambda b: (b + first, 0, 0)),
            pl.BlockSpec((1, groups * heads, own), lambda b: (b + first, 0, 0)),
            pl.BlockSpec(turns.shape, lambda b: (0, 0, 0)),
        ]
        + kv_specs(kv, kv_at)
        + [hbm] * len(into),
        out_specs=[
            pl.BlockSpec((own, width), lambda b: (b + first, 0)),
            pl.BlockSpec((chunks // 2, 1, kv_rows, own), lambda b: (0, b, 0, 0)),
            pl.BlockSpec((chunks // 2, 1, kv_rows, own), lambda b: (0, b, 0, 0)),
        ],
        out_shape=[
            jax.ShapeDtypeStruct((count * own, width), BF),
            jax.ShapeDtypeStruct((chunks // 2, size, kv_rows, own), BF),
            jax.ShapeDtypeStruct((chunks // 2, size, kv_rows, own), BF),
        ],
        scratch_shapes=[
            pltpu.VMEM((chunks, kv_rows, own), BF),
            pltpu.VMEM((kv_rows, own), BF),
            pltpu.VMEM((groups, HD, wide), BF),
            pltpu.VMEM((groups, wide, LANE), BF),
            pltpu.VMEM((groups, HD, wide), BF),
            pltpu.VMEM((groups, wide, LANE), BF),
            pltpu.VMEM((groups, wide, LANE), F32),
        ],
        input_output_aliases={6 + inputs + i: i for i in range(len(into))},
        compiler_params=params(),
        cost_estimate=cost(10**9 * size),
        name="attend_back",
    )(docs, q, do, lse, delta, turns, *kv, *into)


def join_cores(keep, received):
    return [
        (keep[k].astype(F32) + received[k].astype(F32)).astype(BF) for k in range(keep.shape[0])
    ]


def send_keys(summed):
    return [summed[0]] + [shift(summed[k], "seq", k) for k in range(1, len(summed))]


def load_weights(refs, targets, sems):
    copies = []
    slot = 0
    for (source, side, axis), target in zip(refs, targets, strict=True):
        blocks = source.shape[axis] // LANE
        for t in range(blocks):
            to = pl.ds((2 * t + side) * LANE, LANE)
            of = pl.ds(t * LANE, LANE)
            src = source.at[:, of] if axis == 1 else source.at[of]
            dst = target.at[:, to] if axis == 1 else target.at[to]
            copies.append(pltpu.make_async_copy(src, dst, sems.at[slot]))
            slot += 1
    return copies


def put(ref, t, value):
    value = value.astype(BF)
    ref[2 * t], ref[2 * t + 1] = value[:, :LANE], value[:, LANE:]


def wide(ref):
    return jnp.concatenate([ref[i] for i in range(ref.shape[0])], axis=1)


def feed_kernel(
    x_ref, og_ref, ga_ref, o_ref, gain_ref, wo_ref, wgo_ref, wgp_ref, wuo_ref, wup_ref, wdo_ref, wdp_ref,
    out_ref, nt_ref, ogt_ref, act_ref, gg_ref, gu_ref, gh_ref, gat_ref, do_ref, delta_ref, gg2_ref,
    wo, wg, wu, wd, sems,
):
    b = pl.program_id(0)

    @pl.when(b == 0)
    def _():
        copies = [pltpu.make_async_copy(wo_ref, wo, sems.at[sems.shape[0] - 1])]
        copies += load_weights(
            [
                (wgo_ref, 0, 1), (wgp_ref, 1, 1), (wuo_ref, 0, 1), (wup_ref, 1, 1),
                (wdo_ref, 0, 0), (wdp_ref, 1, 0),
            ],
            [wg, wg, wu, wu, wd, wd],
            sems,
        )
        for copy in copies:
            copy.start()
        for copy in copies:
            copy.wait()
        gg2_ref[...] = jnp.zeros(gg2_ref.shape, F32)

    og = og_ref[0]
    heads_out = o_ref[0]
    gain = gain_ref[...]
    hidden = x_ref[0].astype(F32) + mxu(heads_out, wo[...], TN)
    inverse = lax.rsqrt(jnp.mean(hidden * hidden, axis=-1, keepdims=True) + epsilon)
    normed = (hidden * inverse * gain).astype(BF)
    nt_ref[0] = normed.T
    ogt_ref[0] = og.T
    units = wg.shape[1]
    tile = 2 * LANE
    for t in range(units // tile):
        at = slice(t * tile, (t + 1) * tile)
        gate = mxu(normed, wg[:, at], NN)
        up = mxu(normed, wu[:, at], NN)
        grad = ga_ref[:, at].astype(F32)
        sigmoid = 1.0 / (1.0 + jnp.exp(-gate))
        silu = gate * sigmoid
        put(act_ref, t, silu * up)
        put(gu_ref, t, grad * silu)
        put(gg_ref, t, grad * up * (sigmoid + silu * (1.0 - sigmoid)))
    result = mxu(wide(act_ref), wd[...], NN)
    out_ref[0] = (hidden + result).astype(BF)
    grad_normed = mxu(wide(gg_ref), wg[...], NT) + mxu(wide(gu_ref), wu[...], NT)
    scaled = grad_normed * gain
    gg2_ref[...] += jnp.sum(grad_normed * (hidden * inverse), axis=0, keepdims=True)
    mean = jnp.mean(scaled * hidden, axis=-1, keepdims=True)
    grad_hidden = og.astype(F32) + inverse * scaled - hidden * (inverse * inverse * inverse * mean)
    grad_attended = grad_hidden.astype(BF)
    gh_ref[0] = grad_attended
    gat_ref[0] = grad_attended.T
    grad_heads = mxu(wo[...], grad_attended, NT).astype(BF)
    do_ref[0] = grad_heads
    product = grad_heads.astype(F32) * heads_out.astype(F32)
    for h in range(product.shape[0] // HD):
        delta_ref[0, h : h + 1] = jnp.sum(product[h * HD : (h + 1) * HD], axis=0, keepdims=True)


def feed(x, og, slopes, heads_out, gain, wo, wg, wu, wd):
    count, own, width = x.shape
    hd = heads_out.shape[1]
    half = wg[0].shape[1]
    units = 2 * half
    tokens = count * own
    seq = pl.BlockSpec((1, own, width), lambda b: (b, 0, 0))
    column = lambda rows: pl.BlockSpec((1, rows, own), lambda b: (b, 0, 0))
    row = pl.BlockSpec((own, units), lambda b: (b, 0))
    blocks = pl.BlockSpec((units // LANE, own, LANE), lambda b: (0, b, 0))
    hbm = pl.BlockSpec(memory_space=pl.ANY)
    return pl.pallas_call(
        feed_kernel,
        grid=(count,),
        in_specs=[seq, seq, row, column(hd), pl.BlockSpec((1, width), lambda b: (0, 0))] + [hbm] * 7,
        out_specs=[
            seq, column(width), column(width), blocks, blocks, blocks, seq, column(width), column(hd),
            pl.BlockSpec((1, hd // HD, own), lambda b: (b, 0, 0)),
            pl.BlockSpec((1, width), lambda b: (0, 0)),
        ],
        out_shape=[
            jax.ShapeDtypeStruct(x.shape, BF),
            jax.ShapeDtypeStruct((count, width, own), BF),
            jax.ShapeDtypeStruct((count, width, own), BF),
            jax.ShapeDtypeStruct((units // LANE, tokens, LANE), BF),
            jax.ShapeDtypeStruct((units // LANE, tokens, LANE), BF),
            jax.ShapeDtypeStruct((units // LANE, tokens, LANE), BF),
            jax.ShapeDtypeStruct(x.shape, BF),
            jax.ShapeDtypeStruct((count, width, own), BF),
            jax.ShapeDtypeStruct((count, hd, own), BF),
            jax.ShapeDtypeStruct((count, hd // HD, own), F32),
            jax.ShapeDtypeStruct((1, width), F32),
        ],
        scratch_shapes=[
            pltpu.VMEM((hd, width), BF),
            pltpu.VMEM((width, units), BF),
            pltpu.VMEM((width, units), BF),
            pltpu.VMEM((units, width), BF),
            pltpu.SemaphoreType.DMA((6 * (half // LANE) + 1,)),
        ],
        compiler_params=params(),
        cost_estimate=cost(2 * tokens * width * (5 * units + 2 * hd)),
        name="feed",
    )(x, og, slopes, heads_out, gain, wo, *wg, *wu, *wd)


def regroup_rows(value, split):
    if split is None:
        return value
    count_d, count_s = split
    own = value.shape[0] // (count_d * count_s)
    return jnp.concatenate(
        [
            value[(d * count_s + s) * own : (d * count_s + s + 1) * own]
            for s in range(count_s)
            for d in range(count_d)
        ],
        axis=0,
    )


def side_by_side(source, target, sems, slot):
    count, _, own = source.shape
    return [
        pltpu.make_async_copy(
            source.at[i], target.at[:, pl.ds(i * own, own)], sems.at[slot + i]
        )
        for i in range(count)
    ]


def early_kernel(
    split, cut, nt_ref, gg_ref, gu_ref, act_ref, act_next_ref, ogt_ref, gat_ref, o_ref, out_ref,
    rest_ref, nt, ogt, gat, heads_out, stage, landed, load_sems, sends, receives,
):
    t = pl.program_id(0)
    core = lax.axis_index("mp")
    tiles = landed.shape[0]
    tile = 2 * LANE
    pairs, head_tiles = gg_tiles(gg_ref, tiles, heads_out)
    other_core = {"mp": 1 - core}
    loads = []
    for source, target in ((nt_ref, nt), (gat_ref, gat), (o_ref, heads_out), (ogt_ref, ogt)):
        loads.append(side_by_side(source, target, load_sems, len(loads) * nt_ref.shape[0]))

    @pl.when(t == 0)
    def _():
        for copies in loads:
            for copy in copies:
                copy.start()
        barrier = pltpu.get_barrier_semaphore()
        pl.semaphore_signal(barrier, inc=1, device_id=other_core, device_id_type=pl.DeviceIdType.MESH)
        pl.semaphore_wait(barrier, 1)
        for copy in loads[0]:
            copy.wait()

    @pl.when(t == pairs)
    def _():
        for copy in loads[1] + loads[2]:
            copy.wait()

    @pl.when(t == pairs + head_tiles)
    def _():
        for copy in loads[3]:
            copy.wait()

    def send(i):
        return pltpu.make_async_remote_copy(
            src_ref=stage.at[lax.rem(i, 2)],
            dst_ref=landed.at[i],
            send_sem=sends.at[i],
            recv_sem=receives.at[i],
            device_id=other_core,
            device_id_type=pl.DeviceIdType.MESH,
        )

    def deliver(product):
        @pl.when(t < tiles)
        def _():
            @pl.when(t >= 2)
            def _():
                send(t - 2).wait_send()

            stage[lax.rem(t, 2)] = regroup_rows(product(), split).astype(BF)
            send(t).start()

        @pl.when(t >= tiles)
        def _():
            @pl.when(t < tiles + 2)
            def _():
                send(t - 2).wait_send()

            send(t - tiles).wait_recv()
            total = regroup_rows(product(), split) + landed[t - tiles].astype(F32)
            total = total.astype(BF)
            out_ref[...] = jnp.where(t < tiles + cut, total, out_ref[...])
            rest_ref[...] = total

    at = lax.rem(t, tiles)

    @pl.when(at < pairs)
    def _():
        deliver(lambda: mxu(nt[...], jnp.concatenate([gg_ref[0], gu_ref[0]], axis=1), NN))

    @pl.when((at >= pairs) & (at < pairs + head_tiles))
    def _():
        side = jnp.where(t < tiles, 1 - core, core)
        row = pl.multiple_of((side * head_tiles + at - pairs) * tile, tile)
        deliver(lambda: mxu(gat[...], heads_out[pl.ds(row, tile)], NT))

    @pl.when(at >= pairs + head_tiles)
    def _():
        deliver(
            lambda: mxu(ogt[...], jnp.concatenate([act_ref[0], act_next_ref[0]], axis=1), NN)
        )


def gg_tiles(gg_ref, tiles, heads_out):
    head_tiles = heads_out.shape[0] // (4 * LANE)
    return (2 * (tiles - head_tiles)) // 3, head_tiles


def early_grads(nt, gg, gu, act, ogt, gat, heads_out, split):
    count, width, own = nt.shape
    tokens = count * own
    units = gg.shape[0] * LANE
    blocks = units // (2 * LANE)
    tile = 2 * LANE
    hd = heads_out.shape[1]
    head_tiles = hd // (2 * tile)
    down_tiles = (blocks + 1) // 2
    tiles = blocks + head_tiles + down_tiles
    cut = tiles - 4
    rest = units + units // 2 + hd // 2 - cut * tile
    hbm = pl.BlockSpec(memory_space=pl.ANY)
    side = lambda t: jnp.where(t < tiles, 1, 0)

    def pair(t):
        return (2 * jnp.minimum(lax.rem(t, tiles), blocks - 1) + side(t), 0, 0)

    def down(t, shift_by):
        at = jnp.clip(lax.rem(t, tiles) - blocks - head_tiles, 0, down_tiles - 1)
        return (2 * jnp.minimum(2 * at + shift_by, blocks - 1) + side(t), 0, 0)

    block = lambda index: pl.BlockSpec((1, tokens, LANE), index)
    return pl.pallas_call(
        functools.partial(early_kernel, split, cut),
        grid=(2 * tiles,),
        in_specs=[
            hbm,
            block(pair),
            block(pair),
            block(lambda t: down(t, 0)),
            block(lambda t: down(t, 1)),
            hbm,
            hbm,
            hbm,
        ],
        out_specs=[
            pl.BlockSpec((width, tile), lambda t: (0, jnp.clip(t - tiles, 0, cut - 1))),
            pl.BlockSpec((width, tile), lambda t: (0, jnp.maximum(t - tiles - cut, 0))),
        ],
        out_shape=[
            jax.ShapeDtypeStruct((width, cut * tile), BF),
            jax.ShapeDtypeStruct((width, rest), BF),
        ],
        scratch_shapes=[
            pltpu.VMEM((width, tokens), BF),
            pltpu.VMEM((width, tokens), BF),
            pltpu.VMEM((width, tokens), BF),
            pltpu.VMEM((hd, tokens), BF),
            pltpu.VMEM((2, width, tile), BF),
            pltpu.VMEM((tiles, width, tile), BF),
            pltpu.SemaphoreType.DMA((4 * count,)),
            pltpu.SemaphoreType.DMA((tiles,)),
            pltpu.SemaphoreType.DMA((tiles,)),
        ],
        compiler_params=pltpu.CompilerParams(
            vmem_limit_bytes=56 * MIB, collective_id=3, has_side_effects=True
        ),
        cost_estimate=cost(6 * 10**10),
        name="early_grads",
    )(nt, gg, gu, act, act, ogt, gat, heads_out)


def tail_kernel(
    order, x_ref, dq_ref, nt_ref, gain_ref, wq_ref, wkv_ref, cos_ref, sin_ref, gg2_ref,
    nt_all_ref, dq_all_ref, early_ref, near_refs, *refs,
):
    count_d, count_s = lax.axis_size("dp"), lax.axis_size("seq")
    me_d, me_s, core = lax.axis_index("dp"), lax.axis_index("seq"), lax.axis_index("mp")
    (keep_mid, got_mid, keep_end, give_end, update_ref, query_out, small_out, early_out) = refs[:8]
    (
        key_in, sum_mid, sum_end, got_end, query_stage, query_in, query_sum, query_seq, query_part,
        query_dp, early_in, early_own, nt_all, dq_all, load_sems, dw, gg1, small_other, small_in, small_sum, small_seq, small_part,
        small_dp, sends, receives,
    ) = refs[8:]
    rows = query_out.shape[0]
    step = pl.program_id(0)
    other_core = {"mp": 1 - core}
    seq_peers = [{"seq": lax.rem(me_s + k, count_s)} for k in range(1, count_s)]
    dp_peers = [{"dp": lax.rem(me_d + k, count_d)} for k in range(1, count_d)]
    peers = [other_core] + seq_peers + dp_peers
    slots = iter(range(sends.shape[0]))

    def link(source, target, peer):
        slot = next(slots)
        return pltpu.make_async_remote_copy(
            src_ref=source,
            dst_ref=target,
            send_sem=sends.at[slot],
            recv_sem=receives.at[slot],
            device_id=peer,
            device_id_type=pl.DeviceIdType.MESH,
        )

    to_seq = [lax.rem(me_s + k, count_s) for k in range(1, count_s)]
    to_dp = [lax.rem(me_d + k, count_d) for k in range(1, count_d)]
    early_copies = [
        link(early_ref.at[to_dp[k]], early_in.at[k], dp_peers[k]) for k in range(count_d - 1)
    ]
    end_core = link(give_end, got_end, other_core)
    key_copies, at = [], 0
    for part in (sum_mid, sum_end):
        size = part.shape[1]
        key_copies.append(
            [
                link(part.at[k + 1], key_in.at[k, pl.ds(at, size)], seq_peers[k])
                for k in range(count_s - 1)
            ]
        )
        at += size
    query_core = link(query_stage, query_in, other_core)
    query_seqs = [
        link(query_sum.at[to_seq[k]], query_seq.at[k], seq_peers[k]) for k in range(count_s - 1)
    ]
    query_dps = [
        link(query_part.at[to_dp[k]], query_dp.at[k], dp_peers[k]) for k in range(count_d - 1)
    ]
    small_core = link(small_other, small_in, other_core)
    small_seqs = [
        link(small_sum.at[to_seq[k]], small_seq.at[k], seq_peers[k]) for k in range(count_s - 1)
    ]
    small_dps = [
        link(small_part.at[to_dp[k]], small_dp.at[k], dp_peers[k]) for k in range(count_d - 1)
    ]

    def start(copies):
        for copy in copies:
            copy.start()

    def by_seq(total, target):
        for s in range(count_s):
            for d in range(count_d):
                of = (d * count_s + s) * rows
                target[s, d * rows : (d + 1) * rows] = total[of : of + rows].astype(BF)

    def gather(own, copies, arrived):
        total = own.astype(F32)
        for k, copy in enumerate(copies):
            copy.wait()
            total = total + arrived[k].astype(F32)
        return total

    def by_dp(total, target):
        for d in range(count_d):
            target[d] = total[d * rows : (d + 1) * rows].astype(BF)

    loads = side_by_side(nt_all_ref, nt_all, load_sems, 2) + [
        pltpu.make_async_copy(dq_all_ref, dq_all, load_sems.at[0]),
        pltpu.make_async_copy(early_ref.at[me_d], early_own, load_sems.at[1]),
    ]

    def join(mine, got, total):
        for k in range(count_s):
            total[k] = (mine[k].astype(F32) + got[k].astype(F32)).astype(BF)

    def query_product(half):
        size = query_stage.shape[1]
        columns = pl.ds(pl.multiple_of(half * size, size), size)
        return mxu(nt_all[...], dq_all[:, columns], NN)

    @pl.when(step == 0)
    def _():
        barrier = pltpu.get_barrier_semaphore()
        for peer in peers:
            pl.semaphore_signal(barrier, inc=1, device_id=peer, device_id_type=pl.DeviceIdType.MESH)
        pl.semaphore_wait(barrier, len(peers))
        start([end_core])
        join(keep_mid, got_mid, sum_mid)
        start(key_copies[0])
        start(early_copies)
        start(loads)
        end_core.wait()
        join(keep_end, got_end, sum_end)
        start(key_copies[1])
        for load in loads:
            load.wait()
        query_stage[...] = query_product(1 - core).astype(BF)
        start([query_core])
        dw[...] = jnp.zeros(dw.shape, F32)
        gg1[...] = jnp.zeros(gg1.shape, F32)

    @pl.when(step == 1)
    def _():
        product = query_product(core)
        query_core.wait()
        by_seq(product + query_in[...].astype(F32), query_sum)
        start(query_seqs)

    tied = wkv_ref.shape[0] - RD

    def finish(summed):
        turned = rotate_rows(summed[tied:], cos_ref[...], -sin_ref[...])
        dkv = jnp.concatenate([summed[:tied], turned], axis=0).astype(BF)
        grad_normed = mxu(dq_ref[...], wq_ref[...], NN) + mxu(dkv, wkv_ref[...], TN)
        dw[...] += mxu(nt_ref[0], dkv, NT)
        x = x_ref[0].astype(F32)
        inverse = lax.rsqrt(jnp.mean(x * x, axis=-1, keepdims=True) + epsilon)
        scaled = grad_normed * gain_ref[...]
        gg1[...] += jnp.sum(grad_normed * (x * inverse), axis=0, keepdims=True)
        mean = jnp.mean(scaled * x, axis=-1, keepdims=True)
        update = inverse * scaled - x * (inverse * inverse * inverse * mean)
        update_ref[0] = update.astype(BF)

    begin = 0
    for (_, size), terms in zip(order, near_refs):

        @pl.when((step >= begin) & (step < begin + size))
        def _():
            summed = terms[0][0].astype(F32)
            for ref in terms[1:]:
                summed = summed + ref[0].astype(F32)
            finish(summed)

        begin += size

    base = begin
    for part, far in enumerate((sum_mid, sum_end)):
        size = far.shape[1]

        @pl.when(step == begin)
        def _():
            for copy in key_copies[part]:
                copy.wait()

        @pl.when((step >= begin) & (step < begin + size))
        def _():
            at = step - base
            summed = far[0, step - begin].astype(F32)
            for k in range(count_s - 1):
                summed = summed + key_in[k, at].astype(F32)
            finish(summed)

        begin += size

    @pl.when(step == begin - 2)
    def _():
        total = gather(query_sum[me_s], query_seqs, query_seq)
        by_dp(total, query_part)
        start(query_dps)

    @pl.when(step == begin - 1)
    def _():
        width = dw.shape[0]
        pad = jnp.zeros((LANE - RD, width), F32)
        row = lax.broadcasted_iota(jnp.int32, (LANE, width), 0)
        gains = jnp.where(row == RD, gg1[...], 0.0)
        gains = jnp.where(row == RD + 1, gg2_ref[...], gains)
        weights = dw[...]
        rope = jnp.concatenate([weights[:, tied:], jnp.zeros((width, LANE - RD), F32)], axis=1)
        small = rope + gains.T
        half = tied // 2
        first, second = weights[:, :half], weights[:, half:tied]
        mine = jnp.concatenate([jnp.where(core == 0, first, second), small], axis=1)
        other = jnp.concatenate([jnp.where(core == 0, second, first), small], axis=1)
        small_other[...] = other.astype(BF)
        start([small_core])
        small_core.wait()
        by_seq(mine + small_in[...].astype(F32), small_sum)
        start(small_seqs)
        by_dp(gather(small_sum[me_s], small_seqs, small_seq), small_part)
        start(small_dps)
        query_out[...] = gather(query_part[me_d], query_dps, query_dp)
        early_out[...] = gather(early_own[...], early_copies, early_in)
        small_out[...] = gather(small_part[me_d], small_dps, small_dp)


def tail(
    order, x, dq, nt, gain, wq, wkv, cosine, sine_table, grad_gain_two, early, near,
    shares,
):
    count, own, width = x.shape
    count_d, count_s = lax.axis_size("dp"), lax.axis_size("seq")
    rows = width // (count_d * count_s)
    kv_rows = wkv.shape[0]
    tied = kv_rows - RD
    wide = dq.shape[1] // 2
    narrow = tied // 2 + LANE
    middle, end = shares[0].shape, shares[2].shape
    sent = middle[1] + end[1]

    def place(i):
        done, at = 0, i
        for first, size in order:
            at = jnp.where((i >= done) & (i < done + size), first + i - done, at)
            done += size
        return at

    seq = pl.BlockSpec((1, own, width), lambda i: (place(i), 0, 0))
    whole = lambda array: pl.BlockSpec(array.shape, lambda i: (0,) * array.ndim)
    near_specs, done = [], 0
    for (_, size), terms in zip(order, near):
        index = lambda i, done=done, size=size: (jnp.clip(i - done, 0, size - 1), 0, 0)
        near_specs += [pl.BlockSpec((1, kv_rows, own), index)] * len(terms)
        done += size
    fixed = [gain, wq, wkv, cosine, sine_table, grad_gain_two]
    hbm = pl.BlockSpec(memory_space=pl.ANY)
    outs = [
        jax.ShapeDtypeStruct(x.shape, BF),
        jax.ShapeDtypeStruct((rows, wide), F32),
        jax.ShapeDtypeStruct((rows, narrow), F32),
        jax.ShapeDtypeStruct((rows, early.shape[2]), F32),
    ]
    near_all = [term for terms in near for term in terms]

    def kernel(*refs):
        head, rest = refs[:12], refs[12 + len(near_all) :]
        nears = [refs[12 + i * count_s : 12 + (i + 1) * count_s] for i in range(len(near))]
        tail_kernel(order, *head, nears, *rest)

    slots = 3 * (count_d - 1) + 4 * (count_s - 1) + 3
    return pl.pallas_call(
        kernel,
        grid=(count,),
        in_specs=[
            seq,
            pl.BlockSpec((own, dq.shape[1]), lambda i: (place(i), 0)),
            pl.BlockSpec((1, width, own), lambda i: (place(i), 0, 0)),
        ]
        + [whole(array) for array in fixed]
        + [hbm, hbm, hbm]
        + near_specs
        + [whole(array) for array in shares],
        out_specs=[seq] + [whole(out) for out in outs[1:]],
        out_shape=outs,
        scratch_shapes=[
            pltpu.VMEM((count_s - 1, sent, kv_rows, own), BF),
            pltpu.VMEM(middle, BF),
            pltpu.VMEM(end, BF),
            pltpu.VMEM(end, BF),
            pltpu.VMEM((width, wide), BF),
            pltpu.VMEM((width, wide), BF),
            pltpu.VMEM((count_s, count_d * rows, wide), BF),
            pltpu.VMEM((count_s - 1, count_d * rows, wide), BF),
            pltpu.VMEM((count_d, rows, wide), BF),
            pltpu.VMEM((count_d - 1, rows, wide), BF),
            pltpu.VMEM((count_d - 1, rows, early.shape[2]), BF),
            pltpu.VMEM((rows, early.shape[2]), BF),
            pltpu.VMEM((width, count * own), BF),
            pltpu.VMEM(dq.shape, BF),
            pltpu.SemaphoreType.DMA((2 + count,)),
            pltpu.VMEM((width, kv_rows), F32),
            pltpu.VMEM((1, width), F32),
            pltpu.VMEM((width, narrow), BF),
            pltpu.VMEM((width, narrow), BF),
            pltpu.VMEM((count_s, count_d * rows, narrow), BF),
            pltpu.VMEM((count_s - 1, count_d * rows, narrow), BF),
            pltpu.VMEM((count_d, rows, narrow), BF),
            pltpu.VMEM((count_d - 1, rows, narrow), BF),
            pltpu.SemaphoreType.DMA((slots,)),
            pltpu.SemaphoreType.DMA((slots,)),
        ],
        compiler_params=pltpu.CompilerParams(
            vmem_limit_bytes=56 * MIB, collective_id=1, has_side_effects=True
        ),
        cost_estimate=cost(10**8),
        name="tail",
    )(x, dq, nt, *fixed, nt, dq, early, *near_all, *shares)


def turn_tables(cosine, sine_table):
    plain = HD - RD
    one = jnp.ones((cosine.shape[0], plain), F32)
    none = jnp.zeros_like(one)
    quiet = jnp.zeros_like(sine_table)
    straight = jnp.concatenate([one, cosine, cosine], axis=1)
    ahead = jnp.concatenate([none, sine_table, quiet], axis=1)
    behind = jnp.concatenate([none, quiet, -sine_table], axis=1)
    tables = jnp.stack([jnp.concatenate([t, t], axis=1) for t in (straight, ahead, behind)])
    return tables * HD ** (-0.5)


def after(value, *others):
    return lax.optimization_barrier((value, *others))[0]


def on_device_fast(
    inputs, gain_one, w_query, w_tied, w_rope, w_out, gain_two, w_gate, w_up, w_down,
    doc_starts, out_grad,
):
    count, own, width = inputs.shape
    cores = lax.axis_size("mp")
    groups = cores * w_tied.shape[1] // HD
    all_heads = cores * w_query.shape[1] // HD
    heads = all_heads // groups
    mp_index = lax.axis_index("mp")
    split = (lax.axis_size("dp"), lax.axis_size("seq"))
    tied_other, query_other = swap_cores(w_tied), swap_cores(w_query)
    down_other = swap_cores(w_down)
    gain_one_float = gain_one.astype(F32)[None]
    gain_two_float = gain_two.astype(F32)[None]
    cosine, sine_table = rope_tables(my_chunk() * own, own, RD)
    cosine_t, sine_t = cosine.T, sine_table.T
    half = count // 2
    kv, normed_t, q, slopes, queries_weights, keys_weights, kv_near, kv_far = project(
        inputs, out_grad, gain_one_float, (w_query, query_other), (w_tied, tied_other), w_rope,
        (w_down, down_other), cosine_t, sine_t, half,
    )
    kv_late = send_near(kv)
    out_other = swap_cores(after(w_out, kv))
    gate_other, up_other = swap_cores(after(w_gate, kv)), swap_cores(after(w_up, kv))
    span = half - half // 4
    made = attend_forward(doc_starts, q, [kv_near, kv_far], groups, heads, 0, span, 0, ())
    kv_late = send_far([after(part, *made) for part in kv_late])
    made = attend_forward(
        doc_starts, q, [kv_near, kv_far], groups, heads, span, half - span, span, made
    )
    heads_out, lse = attend_forward(doc_starts, q, kv_late, groups, heads, half, half, 0, made)
    out_both = by_core(w_out, after(out_other, lse), 0)
    (
        outputs, normed_two_t, out_grad_t, active, grad_gate, grad_up, grad_hidden, grad_attended_t,
        grad_heads, delta, grad_gain_two,
    ) = feed(
        inputs, out_grad, slopes, heads_out, gain_two_float, out_both, (w_gate, gate_other),
        (w_up, up_other), (w_down, down_other),
    )
    units, head_half = w_gate.shape[1], w_out.shape[0]
    first_sum, rest_sum = early_grads(
        normed_two_t, grad_gate, grad_up, active, out_grad_t, grad_attended_t, heads_out, split
    )
    first_sum, rest_sum, grad_heads = lax.optimization_barrier((first_sum, rest_sum, grad_heads))
    first_sum = lax.psum_scatter(first_sum, "seq", scatter_dimension=0, tiled=True)

    turns = turn_tables(cosine, sine_table)
    quarter = half // 2
    backward = [
        (half, half, kv_late, 0),
        (quarter, half - quarter, [kv_near, kv_far], quarter),
        (0, quarter, [kv_near, kv_far], 0),
    ]
    rest_sum = rest_sum.reshape(split[1], split[0], -1, rest_sum.shape[1])
    rest_sum = add_up(send_steps(rest_sum, "dp", 1)).astype(BF)
    rest_terms = send_steps(rest_sum, "seq", 0)
    dq, near, shares = (), [], []
    for part, (at, size, kv_part, kv_at) in enumerate(backward):
        need = near[0][:1] if part == 2 else []
        made_dq, keep, give = attend_backward(
            doc_starts, after(q, *need), grad_heads, lse, delta, turns, kv_part, groups, heads, at,
            size, kv_at, dq,
        )
        dq = (made_dq,)
        if part == 0:
            first_shares = (keep, swap_cores(after(give, rest_sum)))
        if part == 1:
            give = after(give, *rest_terms)
            near.append(send_keys(join_cores(*first_shares)))
            shares = [keep, swap_cores(give)]
        if part == 2:
            shares += [keep, give]
    early = first_sum.reshape(split[0], -1, first_sum.shape[1])
    order = [span[:2] for span in backward]
    update, query_sum, small_sum, first_sum = tail(
        order, inputs, dq[0], normed_t, gain_one_float, queries_weights, keys_weights,
        cosine_t, sine_t, grad_gain_two, early, near,
        shares,
    )
    grad_inputs = grad_hidden.astype(F32) + update.astype(F32)
    half_tied = groups * HD // cores
    late_sum, small_sum = small_sum[:, :half_tied], small_sum[:, half_tied:]
    rows = small_sum.shape[0] // cores
    small_sum = lax.dynamic_slice_in_dim(small_sum, mp_index * rows, rows, 0)
    pairs = first_sum[:, : 2 * units].reshape(first_sum.shape[0], units // LANE, 2, LANE)
    gate_sum = pairs[:, :, 0].reshape(-1, units)
    up_sum = pairs[:, :, 1].reshape(-1, units)
    out_sum = first_sum[:, 2 * units : 2 * units + head_half]
    down_sum = jnp.concatenate([first_sum[:, 2 * units + head_half :], add_up(rest_terms)], axis=1)
    return (
        outputs,
        grad_inputs,
        small_sum[:, RD],
        query_sum,
        late_sum,
        small_sum[:, :RD],
        out_sum.T,
        small_sum[:, RD + 1],
        gate_sum,
        up_sum,
        down_sum.T,
    )


def solution(mesh):
    in_specs = (
        P("dp", ("seq", "mp"), None),
        P(),
        P(None, "mp"),
        P(None, "mp"),
        P(),
        P("mp", None),
        P(),
        P(None, "mp"),
        P(None, "mp"),
        P("mp", None),
        P("dp", None),
        P("dp", ("seq", "mp"), None),
    )
    out_specs = (
        P("dp", ("seq", "mp"), None),
        P("dp", ("seq", "mp"), None),
        P(("dp", "seq", "mp")),
        P(("dp", "seq"), "mp"),
        P(("dp", "seq"), "mp"),
        P(("dp", "seq", "mp"), None),
        P("mp", ("dp", "seq")),
        P(("dp", "seq", "mp")),
        P(("dp", "seq"), "mp"),
        P(("dp", "seq"), "mp"),
        P("mp", ("dp", "seq")),
    )

    def local(inputs, *rest):
        step = on_device_fast if inputs.shape[1] % (2 * LANE) == 0 else on_device
        return step(inputs, *rest)

    return jax.shard_map(
        local, mesh=mesh, in_specs=in_specs, out_specs=out_specs, check_vma=False
    )
```

profile of v0, /device:TPU:0, one launch (start us, length us, event | category | flops | bytes accessed | tf_op | source)
XLA Modules:
  0.0 493.1 jit_solution(8429696551416320384)
XLA Ops:
  7.2 0.5 collective-permute-start.2
  7.8 0.4 collective-permute-start.1
  8.3 1.3 broadcast_in_dim.60
  9.6 1.7 copy.31.wr_ref
  11.2 1.3 broadcast_in_dim.61
  12.5 0.8 multiply_sine_fusion.1
  13.3 1.5 collective-permute-done.1.wtp_ref
  14.8 0.6 copy-done.18
  15.4 0.9 copy-done.17
  16.4 39.8 %project.1 = (bf16[4,288,256]{2,1,0:T(8,128)(2,1)}, bf16[8,1024,256]{2,1,0:T(8,128)(2,1)}, bf16[8,1024,256]{2,1,0:T(8,128)(2,1)}, bf16[2048,2816]{1,0:T(8,128)(2...) custom-call(bf16[8,256,1024]{2,1,0:T(8,128)(2,1)} %refs_0_.1, ...), custom_call_target="tpu_custom_call" | custom-call | flops 30000001024 | tf_op jit(solution)/shard_map/project/pallas_call | solution.py:534
  56.2 2.4 collective-permute-start.5
  58.6 0.6 collective-permute-start.4
  59.1 0.5 collective-permute-start.3
  59.7 7.2 %attend.3 = (bf16[8,1024,256]{2,1,0:T(8,128)(2,1)}, f32[8,4,1024]{2,1,0:T(4,128)}) custom-call(s32[8,8]{1,0:T(8,128)} %docs_ref.11, bf16[8,1024,256]{2,1,0:T(8,128)(2,1)} %get-tuple-element.101.q_ref, bf16[4,4,288,256]{3,2,1,0:T(8,128)(2,1)} %get-tuple-element.68.refs_0_, bf16[4,4,288,256]{3,2,1,0:T(8,128)(2,1)} %get-tuple-element.69.refs_1_), custom_call_target="tpu_custom_call" | custom-call | flops 30000001024 | tf_op jit(solution)/shard_map/attend/pallas_call | solution.py:758
  66.8 4.8 collective-permute-start.6
  71.7 1.0 collective-permute-done.5
  72.7 14.1 %collective-permute-done.4 = bf16[4,288,256]{2,1,0:T(8,128)(2,1)} collective-permute-done((bf16[4,288,256]{2,1,0:T(8,128)(2,1)}, bf16[4,288,256]{2,1,0:T(8,128)(2,1)}, u32[]{:S(2)}, u32[]{:S(2)}) %collective-permute-start.4) | collective-permute-done | bytes 589856 | tf_op jit(solution)/shard_map/ppermute | solution.py:367
  86.8 0.5 collective-permute-start.8
  87.3 4.3 attend.4
  91.7 2.3 collective-permute-start.11
  94.0 8.9 %attend.5 = (bf16[8,1024,256]{2,1,0:T(8,128)(2,1)}, f32[8,4,1024]{2,1,0:T(4,128)}) custom-call(s32[8,8]{1,0:T(8,128)} %docs_ref.11, bf16[8,1024,256]{2,1,0:T(8,128)(2,1)} %get-tuple-element.101.q_ref, bf16[1,4,288,256]{3,2,1,0:T(8,128)(2,1)} %bitcast.1.refs_0_, ...), custom_call_target="tpu_custom_call", output_to_operand_aliasing={{0}: (10, {}), {1}: (11, {})} | custom-call | flops 40000000000 | tf_op jit(solution)/shard_map/attend/pallas_call | solution.py:758
  102.9 0.1 broadcast_select_fusion.1
  103.1 1.6 pad_maximum_fusion.wo_ref
  104.6 87.8 %feed.1 = (bf16[8,256,1024]{2,1,0:T(8,128)(2,1)}, bf16[8,1024,256]{2,1,0:T(8,128)(2,1)}, bf16[8,1024,256]{2,1,0:T(8,128)(2,1)}, bf16[22,2048,128]{2,1,0:T(8,128)...) custom-call(bf16[8,256,1024]{2,1,0:T(8,128)(2,1)} %refs_0_.1, ...), custom_call_target="tpu_custom_call" | custom-call | flops 67645734912 | tf_op jit(solution)/shard_map/feed/pallas_call | solution.py:1086
  192.4 64.4 %early_grads.1 = (bf16[1024,3840]{1,0:T(8,128)(2,1)}, bf16[1024,896]{1,0:T(8,128)(2,1)}) custom-call(bf16[8,1024,256]{2,1,0:T(8,128)(2,1)} %get-tuple-element.86.nt_ref, bf16[22,2048,128]{2,1,0:T(8,128)(2,1)} %get-tuple-element.87.gg_ref, bf16[22,2048,128]{2,1,0:T(8,128)(2,1)} %get-tuple-element.88.gu_ref, ...), custom_call_target="tpu_custom_call" | custom-call | flops 60000002048 | tf_op jit(solution)/shard_map/early_grads/pallas_call | solution.py:1260
  256.9 0.6 copy-done.12
  257.5 0.5 multiply_cosine_fusion
  258.0 0.2 concatenate.23
  258.3 0.2 concatenate.24
  258.6 0.2 concatenate.22
  258.9 0.1 dynamic-slice_bitcast_fusion.2
  259.0 0.2 collective-permute-start.13
  259.2 3.3 collective-permute-start.14
  262.5 2.1 collective-permute-start.15
  264.6 0.8 maximum_multiply_fusion.rot_ref
  265.4 20.5 %attend_back.3 = (bf16[2048,1024]{1,0:T(8,128)(2,1)}, bf16[4,4,288,256]{3,2,1,0:T(8,128)(2,1)}, bf16[4,4,288,256]{3,2,1,0:T(8,128)(2,1)}) custom-call(s32[8,8]{1,0:T(8,128)} %docs_ref.11, bf16[8,1024,256]{2,1,0:T(8,128)(2,1)} %get-tuple-element.101.q_ref, bf16[8,1024,256]{2,1,0:T(8,128)(2,1)} %get-tuple-element.95.do_ref, ...), custom_call_target="tpu_custom_call" | custom-call | flops 4000000000 | tf_op jit(solution)/shard_map/attend_back/pallas_call | solution.py:941
  285.9 7.2 %collective-permute-done.14 = bf16[4,64,896]{2,1,0:T(8,128)(2,1)S(1)} collective-permute-done((bf16[4,64,896]{2,1,0:T(8,128)(2,1)S(1)}, bf16[4,64,896]{2,1,0:T(8,128)(2,1)S(1)}, u32[]{:S(2)}, u32[]{:S(2)}) %collective-permute-start.14) | collective-permute-done | bytes 458784 | tf_op jit(solution)/shard_map/ppermute | solution.py:367
  293.1 0.2 fusion.2
  293.3 5.2 %collective-permute-start.16 = (bf16[4,4,288,256]{3,2,1,0:T(8,128)(2,1)}, bf16[4,4,288,256]{3,2,1,0:T(8,128)(2,1)S(1)}, u32[]{:S(2)}, u32[]{:S(2)}) collective-permute-start(bf16[4,4,288,256]{3,2,1,0:T(8,128)(2,1)} %get-tuple-element.100), channel_id=1, source_target_pairs={{0,1},{1,0},{2,3},{3,2},{4,5},{5,4},{6,7},{7,6},{8,9},{9,8},{10,11... | collective-permute-start | bytes 7077896 | tf_op jit(solution)/shard_map/ppermute | solution.py:362
  298.6 15.5 %collective-permute-start.20 = (bf16[64,896]{1,0:T(8,128)(2,1)S(1)}, bf16[64,896]{1,0:T(8,128)(2,1)S(1)}, u32[]{:S(2)}, u32[]{:S(2)}) collective-permute-start(bf16[64,896]{1,0:T(8,128)(2,1)S(1)} %get-tuple-element.136), channel_id=1, source_target_pairs={{0,2},{2,4},{4,6},{6,0},{1,3},{3,5},{5,7},{7,1},{8,10},{10,12},{12... | collective-permute-start | bytes 344072 | tf_op jit(solution)/shard_map/ppermute | solution.py:367
  314.1 29.4 %collective-permute-start.21 = (bf16[64,896]{1,0:T(8,128)(2,1)S(1)}, bf16[64,896]{1,0:T(8,128)(2,1)S(1)}, u32[]{:S(2)}, u32[]{:S(2)}) collective-permute-start(bf16[64,896]{1,0:T(8,128)(2,1)S(1)} %get-tuple-element.138), channel_id=1, source_target_pairs={{0,4},{2,6},{4,0},{6,2},{1,5},{3,7},{5,1},{7,3},{8,12},{10,14},{12... | collective-permute-start | bytes 344072 | tf_op jit(solution)/shard_map/ppermute | solution.py:367
  343.5 12.0 %attend_back.4 = (bf16[2048,1024]{1,0:T(8,128)(2,1)}, bf16[4,2,288,256]{3,2,1,0:T(8,128)(2,1)}, bf16[4,2,288,256]{3,2,1,0:T(8,128)(2,1)}) custom-call(s32[8,8]{1,0:T(8,128)} %docs_ref.11, bf16[8,1024,256]{2,1,0:T(8,128)(2,1)} %get-tuple-element.101.q_ref, bf16[8,1024,256]{2,1,0:T(8,128)(2,1)} %get-tuple-element.95.do_ref, ...), custom_call_target="tpu_custom_call", output_to_operand_aliasing={{0}: (8, {})} | custom-call | flops 2000000000 | tf_op jit(solution)/shard_map/attend_back/pallas_call | solution.py:941
  355.5 0.7 convert_add_fusion.2
  356.3 4.4 collective-permute-start.23
  360.7 1.9 fusion.6
  362.6 7.4 %collective-permute-start.17 = (bf16[4,288,256]{2,1,0:T(8,128)(2,1)}, bf16[4,288,256]{2,1,0:T(8,128)(2,1)S(1)}, u32[]{:S(2)}, u32[]{:S(2)}) collective-permute-start(bf16[4,288,256]{2,1,0:T(8,128)(2,1)} %get-tuple-element.127), channel_id=1, source_target_pairs={{0,2},{2,4},{4,6},{6,0},{1,3},{3,5},{5,7},{7,1},{8,10},{10,12},{12... | collective-permute-start | bytes 1769480 | tf_op jit(solution)/shard_map/ppermute | solution.py:367
  370.0 8.8 %collective-permute-start.18 = (bf16[4,288,256]{2,1,0:T(8,128)(2,1)}, bf16[4,288,256]{2,1,0:T(8,128)(2,1)S(1)}, u32[]{:S(2)}, u32[]{:S(2)}) collective-permute-start(bf16[4,288,256]{2,1,0:T(8,128)(2,1)} %get-tuple-element.126), channel_id=1, source_target_pairs={{0,4},{2,6},{4,0},{6,2},{1,5},{3,7},{5,1},{7,3},{8,12},{10,14},{12... | collective-permute-start | bytes 1769480 | tf_op jit(solution)/shard_map/ppermute | solution.py:367
  378.8 2.9 collective-permute-start.19
  381.8 11.4 %attend_back.5 = (bf16[2048,1024]{1,0:T(8,128)(2,1)}, bf16[4,2,288,256]{3,2,1,0:T(8,128)(2,1)}, bf16[4,2,288,256]{3,2,1,0:T(8,128)(2,1)}) custom-call(s32[8,8]{1,0:T(8,128)} %docs_ref.11, bf16[8,1024,256]{2,1,0:T(8,128)(2,1)} %get-tuple-element.101.q_ref, bf16[8,1024,256]{2,1,0:T(8,128)(2,1)} %get-tuple-element.95.do_ref, ...), custom_call_target="tpu_custom_call", output_to_operand_aliasing={{0}: (8, {})} | custom-call | flops 2000000000 | tf_op jit(solution)/shard_map/attend_back/pallas_call | solution.py:941
  393.2 11.3 %collective-permute-done.18.refs_14_ = bf16[4,288,256]{2,1,0:T(8,128)(2,1)S(1)} collective-permute-done((bf16[4,288,256]{2,1,0:T(8,128)(2,1)}, bf16[4,288,256]{2,1,0:T(8,128)(2,1)S(1)}, u32[]{:S(2)}, u32[]{:S(2)}) %collective-permute-start.18) | collective-permute-done | bytes 589856 | tf_op jit(solution)/shard_map/ppermute | solution.py:367
  404.5 1.9 collective-permute-done.19.refs_15_
  406.4 0.8 copy-done.8
  407.3 61.5 %tail.1 = (bf16[8,256,1024]{2,1,0:T(8,128)(2,1)}, f32[64,512]{1,0:T(8,128)}, f32[64,256]{1,0:T(8,128)}, f32[64,3840]{1,0:T(8,128)}) custom-call(bf16[8,256,1024]{2,1,0:T(8,128)(2,1)} %refs_0_.1, bf16[2048,1024]{1,0:T(8,128)(2,1)} %get-tuple-element.104.refs_1_.refs_10_, bf16[8,1024,256]{2,1,0:T(8,128)(2,1)} %get-tuple-element.105.refs_2_.refs_9_, ...), custom_call_target="tpu_custom_call" | custom-call | flops 100000000 | tf_op jit(solution)/shard_map/tail/pallas_call | solution.py:1547
  468.8 1.7 fusion.8
  470.5 1.2 slice.68
  471.6 0.4 reshape.62
  472.0 1.9 slice_reduce_fusion
  474.0 0.6 fusion.9
  474.6 0.8 maximum_bitcast_fusion
  475.4 1.1 copy_bitcast_fusion
  476.4 7.6 %convert_add_fusion = f32[8,256,1024]{2,1,0:T(8,128)} fusion(bf16[8,256,1024]{2,1,0:T(8,128)(2,1)} %get-tuple-element.115, bf16[8,256,1024]{2,1,0:T(8,128)(2,1)S(1)} %copy-done), kind=kLoop, calls=%fused_computation | loop fusion | flops 6291456 | bytes 16777216 | tf_op jit(solution)/shard_map/add | solution.py:1692
  484.0 0.6 constant_dynamic-slice_fusion
  484.6 0.7 dynamic-slice_reduce_fusion
  485.4 0.7 copy.44
  (67 shorter events, 0.6 us)
Async XLA Ops:
  7.2 399.2 %reduce-scatter.2.cloned.1.call-start = ((), (), s32[]{:S(2)}) async-start(), calls=%async_computation.1 | async-start | bytes 9830400 | tf_op jit(solution)/shard_map/reduce_scatter | solution.py:1657
  7.2 7.6 %collective-permute-start.2 = (bf16[1408,1024]{1,0:T(8,128)(2,1)}, bf16[1408,1024]{1,0:T(8,128)(2,1)S(1)}, u32[]{:S(2)}, u32[]{:S(2)}) collective-permute-start(bf16[1408,1024]{1,0:T(8,128)(2,1)} %wdo_ref.3), channel_id=1, source_target_pairs={{0,1},{1,0},{2,3},{3,2},{4,5},{5,4},{6,7},{7,6},{8,9},{9,8},{10,11... | collective-permute-start | bytes 8650760 | tf_op jit(solution)/shard_map/ppermute | solution.py:362
  7.7 7.0 %collective-permute-start = (bf16[1024,512]{1,0:T(8,128)(2,1)}, bf16[1024,512]{1,0:T(8,128)(2,1)}, u32[]{:S(2)}, u32[]{:S(2)}) collective-permute-start(bf16[1024,512]{1,0:T(8,128)(2,1)} %wqo_ref.1), channel_id=1, source_target_pairs={{0,1},{1,0},{2,3},{3,2},{4,5},{5,4},{6,7},{7,6},{8,9},{9,8},{10,11... | collective-permute-start | bytes 3145736 | tf_op jit(solution)/shard_map/ppermute | solution.py:362
  7.8 6.9 %collective-permute-start.1 = (bf16[1024,128]{1,0:T(8,128)(2,1)}, bf16[1024,128]{1,0:T(8,128)(2,1)S(1)}, u32[]{:S(2)}, u32[]{:S(2)}) collective-permute-start(bf16[1024,128]{1,0:T(8,128)(2,1)} %wto_ref.1), channel_id=1, source_target_pairs={{0,1},{1,0},{2,3},{3,2},{4,5},{5,4},{6,7},{7,6},{8,9},{9,8},{10,11... | collective-permute-start | bytes 786440 | tf_op jit(solution)/shard_map/ppermute | solution.py:362
  8.3 47.9 %copy-start.11 = (f32[256]{0:T(256)}, f32[256]{0:T(256)S(1)}, u32[]{:S(2)}) copy-start(f32[256]{0:T(256)S(1)} %add_convert_fusion.4) | copy-start | bytes 3076
  8.3 47.9 %copy-start.13 = (f32[16]{0:T(128)}, f32[16]{0:T(128)S(1)}, u32[]{:S(2)}) copy-start(f32[16]{0:T(128)S(1)} %multiply_power_fusion) | copy-start | bytes 196
  14.7 0.7 copy-start.18
  14.8 1.6 copy-start.17
  56.2 16.5 %collective-permute-start.5 = (bf16[4,288,256]{2,1,0:T(8,128)(2,1)}, bf16[4,288,256]{2,1,0:T(8,128)(2,1)}, u32[]{:S(2)}, u32[]{:S(2)}) collective-permute-start(bf16[4,288,256]{2,1,0:T(8,128)(2,1)} %get-tuple-element.72), channel_id=1, source_target_pairs={{0,6},{2,0},{4,2},{6,4},{1,7},{3,1},{5,3},{7,5},{8,14},{10,8},{12,... | collective-permute-start | bytes 1769480 | tf_op jit(solution)/shard_map/ppermute | solution.py:367
  58.6 28.3 %collective-permute-start.4 = (bf16[4,288,256]{2,1,0:T(8,128)(2,1)}, bf16[4,288,256]{2,1,0:T(8,128)(2,1)}, u32[]{:S(2)}, u32[]{:S(2)}) collective-permute-start(bf16[4,288,256]{2,1,0:T(8,128)(2,1)} %get-tuple-element.72), channel_id=1, source_target_pairs={{0,4},{2,6},{4,0},{6,2},{1,5},{3,7},{5,1},{7,3},{8,12},{10,14},{12... | collective-permute-start | bytes 1769480 | tf_op jit(solution)/shard_map/ppermute | solution.py:367
  59.1 27.7 %collective-permute-start.3 = (bf16[4,288,256]{2,1,0:T(8,128)(2,1)}, bf16[4,288,256]{2,1,0:T(8,128)(2,1)}, u32[]{:S(2)}, u32[]{:S(2)}) collective-permute-start(bf16[4,288,256]{2,1,0:T(8,128)(2,1)} %get-tuple-element.72), channel_id=1, source_target_pairs={{0,2},{2,4},{4,6},{6,0},{1,3},{3,5},{5,7},{7,1},{8,10},{10,12},{12... | collective-permute-start | bytes 1769480 | tf_op jit(solution)/shard_map/ppermute | solution.py:367
  59.7 11.9 %copy-start.4 = (bf16[512,1024]{1,0:T(8,128)(2,1)S(1)}, bf16[512,1024]{1,0:T(8,128)(2,1)}, u32[]{:S(2)}) copy-start(bf16[512,1024]{1,0:T(8,128)(2,1)} %param.17) | copy-start | bytes 3145732
  66.8 24.8 %copy-start.15 = (bf16[1024,1408]{1,0:T(8,128)(2,1)S(1)}, bf16[1024,1408]{1,0:T(8,128)(2,1)}, u32[]{:S(2)}) copy-start(bf16[1024,1408]{1,0:T(8,128)(2,1)} %wgo_ref.1) | copy-start | bytes 8650756
  66.8 27.1 %copy-start.16 = (bf16[1024,1408]{1,0:T(8,128)(2,1)S(1)}, bf16[1024,1408]{1,0:T(8,128)(2,1)}, u32[]{:S(2)}) copy-start(bf16[1024,1408]{1,0:T(8,128)(2,1)} %wuo_ref.1) | copy-start | bytes 8650756
  66.8 24.8 %collective-permute-start.6 = (bf16[4,288,256]{2,1,0:T(8,128)(2,1)}, bf16[4,288,256]{2,1,0:T(8,128)(2,1)}, u32[]{:S(2)}, u32[]{:S(2)}) collective-permute-start(bf16[4,288,256]{2,1,0:T(8,128)(2,1)} %get-tuple-element.72), channel_id=1, source_target_pairs={{0,1},{1,0},{2,3},{3,2},{4,5},{5,4},{6,7},{7,6},{8,9},{9,8},{10,11... | collective-permute-start | bytes 1769480 | tf_op jit(solution)/shard_map/ppermute | solution.py:362
  71.6 31.3 %collective-permute-start.10 = (bf16[512,1024]{1,0:T(8,128)(2,1)S(1)}, bf16[512,1024]{1,0:T(8,128)(2,1)S(1)}, u32[]{:S(2)}, u32[]{:S(2)}) collective-permute-start(bf16[512,1024]{1,0:T(8,128)(2,1)S(1)} %copy-done.4), channel_id=1, source_target_pairs={{0,1},{1,0},{2,3},{3,2},{4,5},{5,4},{6,7},{7,6},{8,9},{9,8},{10,11... | collective-permute-start | bytes 3145736 | tf_op jit(solution)/shard_map/ppermute | solution.py:362
  86.8 7.1 %collective-permute-start.9 = (bf16[4,288,256]{2,1,0:T(8,128)(2,1)}, bf16[4,288,256]{2,1,0:T(8,128)(2,1)}, u32[]{:S(2)}, u32[]{:S(2)}) collective-permute-start(bf16[4,288,256]{2,1,0:T(8,128)(2,1)} %collective-permute-done.5), channel_id=1, source_target_pairs={{0,1},{1,0},{2,3},{3,2},{4,5},{5,4},{6,7},{7,6},{8,9},{9,8},{10,11... | collective-permute-start | bytes 1769480 | tf_op jit(solution)/shard_map/ppermute | solution.py:362
  86.8 7.2 %collective-permute-start.8 = (bf16[4,288,256]{2,1,0:T(8,128)(2,1)}, bf16[4,288,256]{2,1,0:T(8,128)(2,1)}, u32[]{:S(2)}, u32[]{:S(2)}) collective-permute-start(bf16[4,288,256]{2,1,0:T(8,128)(2,1)} %collective-permute-done.4), channel_id=1, source_target_pairs={{0,1},{1,0},{2,3},{3,2},{4,5},{5,4},{6,7},{7,6},{8,9},{9,8},{10,11... | collective-permute-start | bytes 1769480 | tf_op jit(solution)/shard_map/ppermute | solution.py:362
  87.3 6.7 %collective-permute-start.7 = (bf16[4,288,256]{2,1,0:T(8,128)(2,1)}, bf16[4,288,256]{2,1,0:T(8,128)(2,1)}, u32[]{:S(2)}, u32[]{:S(2)}) collective-permute-start(bf16[4,288,256]{2,1,0:T(8,128)(2,1)} %collective-permute-done.3), channel_id=1, source_target_pairs={{0,1},{1,0},{2,3},{3,2},{4,5},{5,4},{6,7},{7,6},{8,9},{9,8},{10,11... | collective-permute-start | bytes 1769480 | tf_op jit(solution)/shard_map/ppermute | solution.py:362
  91.7 13.0 %collective-permute-start.11 = (bf16[1024,1408]{1,0:T(8,128)(2,1)S(1)}, bf16[1024,1408]{1,0:T(8,128)(2,1)}, u32[]{:S(2)}, u32[]{:S(2)}) collective-permute-start(bf16[1024,1408]{1,0:T(8,128)(2,1)S(1)} %copy-done.15), channel_id=1, source_target_pairs={{0,1},{1,0},{2,3},{3,2},{4,5},{5,4},{6,7},{7,6},{8,9},{9,8},{10,11... | collective-permute-start | bytes 8650760 | tf_op jit(solution)/shard_map/ppermute | solution.py:362
  93.9 10.7 %collective-permute-start.12 = (bf16[1024,1408]{1,0:T(8,128)(2,1)S(1)}, bf16[1024,1408]{1,0:T(8,128)(2,1)}, u32[]{:S(2)}, u32[]{:S(2)}) collective-permute-start(bf16[1024,1408]{1,0:T(8,128)(2,1)S(1)} %copy-done.16), channel_id=1, source_target_pairs={{0,1},{1,0},{2,3},{3,2},{4,5},{5,4},{6,7},{7,6},{8,9},{9,8},{10,11... | collective-permute-start | bytes 8650760 | tf_op jit(solution)/shard_map/ppermute | solution.py:362
  256.8 0.7 copy-start.12
  256.8 0.7 copy-start.14
  256.8 2.0 copy-start.2
  259.0 26.9 %collective-permute-start.13 = (bf16[4,64,896]{2,1,0:T(8,128)(2,1)S(1)}, bf16[4,64,896]{2,1,0:T(8,128)(2,1)S(1)}, u32[]{:S(2)}, u32[]{:S(2)}) collective-permute-start(bf16[4,64,896]{2,1,0:T(8,128)(2,1)S(1)} %get-tuple-element.131), channel_id=1, source_target_pairs={{0,8},{8,16},{16,24},{24,0},{1,9},{9,17},{17,25},{25,1},{2,10},{10... | collective-permute-start | bytes 1376264 | tf_op jit(solution)/shard_map/ppermute | solution.py:367
  259.2 33.8 %collective-permute-start.14 = (bf16[4,64,896]{2,1,0:T(8,128)(2,1)S(1)}, bf16[4,64,896]{2,1,0:T(8,128)(2,1)S(1)}, u32[]{:S(2)}, u32[]{:S(2)}) collective-permute-start(bf16[4,64,896]{2,1,0:T(8,128)(2,1)S(1)} %get-tuple-element.133), channel_id=1, source_target_pairs={{0,16},{8,24},{16,0},{24,8},{1,17},{9,25},{17,1},{25,9},{2,18},{10... | collective-permute-start | bytes 1376264 | tf_op jit(solution)/shard_map/ppermute | solution.py:367
  262.5 30.6 %collective-permute-start.15 = (bf16[4,64,896]{2,1,0:T(8,128)(2,1)S(1)}, bf16[4,64,896]{2,1,0:T(8,128)(2,1)S(1)}, u32[]{:S(2)}, u32[]{:S(2)}) collective-permute-start(bf16[4,64,896]{2,1,0:T(8,128)(2,1)S(1)} %get-tuple-element.132), channel_id=1, source_target_pairs={{0,24},{8,0},{16,8},{24,16},{1,25},{9,1},{17,9},{25,17},{2,26},{10... | collective-permute-start | bytes 1376264 | tf_op jit(solution)/shard_map/ppermute | solution.py:367
  293.3 67.4 %collective-permute-start.16 = (bf16[4,4,288,256]{3,2,1,0:T(8,128)(2,1)}, bf16[4,4,288,256]{3,2,1,0:T(8,128)(2,1)S(1)}, u32[]{:S(2)}, u32[]{:S(2)}) collective-permute-start(bf16[4,4,288,256]{3,2,1,0:T(8,128)(2,1)} %get-tuple-element.100), channel_id=1, source_target_pairs={{0,1},{1,0},{2,3},{3,2},{4,5},{5,4},{6,7},{7,6},{8,9},{9,8},{10,11... | collective-permute-start | bytes 7077896 | tf_op jit(solution)/shard_map/ppermute | solution.py:362
  298.6 56.9 %collective-permute-start.20 = (bf16[64,896]{1,0:T(8,128)(2,1)S(1)}, bf16[64,896]{1,0:T(8,128)(2,1)S(1)}, u32[]{:S(2)}, u32[]{:S(2)}) collective-permute-start(bf16[64,896]{1,0:T(8,128)(2,1)S(1)} %get-tuple-element.136), channel_id=1, source_target_pairs={{0,2},{2,4},{4,6},{6,0},{1,3},{3,5},{5,7},{7,1},{8,10},{10,12},{12... | collective-permute-start | bytes 344072 | tf_op jit(solution)/shard_map/ppermute | solution.py:367
  314.1 41.4 %collective-permute-start.21 = (bf16[64,896]{1,0:T(8,128)(2,1)S(1)}, bf16[64,896]{1,0:T(8,128)(2,1)S(1)}, u32[]{:S(2)}, u32[]{:S(2)}) collective-permute-start(bf16[64,896]{1,0:T(8,128)(2,1)S(1)} %get-tuple-element.138), channel_id=1, source_target_pairs={{0,4},{2,6},{4,0},{6,2},{1,5},{3,7},{5,1},{7,3},{8,12},{10,14},{12... | collective-permute-start | bytes 344072 | tf_op jit(solution)/shard_map/ppermute | solution.py:367
  343.5 12.0 %collective-permute-start.22 = (bf16[64,896]{1,0:T(8,128)(2,1)S(1)}, bf16[64,896]{1,0:T(8,128)(2,1)S(1)}, u32[]{:S(2)}, u32[]{:S(2)}) collective-permute-start(bf16[64,896]{1,0:T(8,128)(2,1)S(1)} %get-tuple-element.137), channel_id=1, source_target_pairs={{0,6},{2,0},{4,2},{6,4},{1,7},{3,1},{5,3},{7,5},{8,14},{10,8},{12,... | collective-permute-start | bytes 344072 | tf_op jit(solution)/shard_map/ppermute | solution.py:367
  343.5 17.1 %copy-start.1 = (bf16[4,4,288,256]{3,2,1,0:T(8,128)(2,1)S(1)}, bf16[4,4,288,256]{3,2,1,0:T(8,128)(2,1)}, u32[]{:S(2)}) copy-start(bf16[4,4,288,256]{3,2,1,0:T(8,128)(2,1)} %get-tuple-element.97) | copy-start | bytes 7077892
  356.3 36.9 %collective-permute-start.23 = (bf16[4,2,288,256]{3,2,1,0:T(8,128)(2,1)}, bf16[4,2,288,256]{3,2,1,0:T(8,128)(2,1)S(1)}, u32[]{:S(2)}, u32[]{:S(2)}) collective-permute-start(bf16[4,2,288,256]{3,2,1,0:T(8,128)(2,1)} %get-tuple-element.112), channel_id=1, source_target_pairs={{0,1},{1,0},{2,3},{3,2},{4,5},{5,4},{6,7},{7,6},{8,9},{9,8},{10,11... | collective-permute-start | bytes 3538952 | tf_op jit(solution)/shard_map/ppermute | solution.py:362
  362.6 30.6 %collective-permute-start.17 = (bf16[4,288,256]{2,1,0:T(8,128)(2,1)}, bf16[4,288,256]{2,1,0:T(8,128)(2,1)S(1)}, u32[]{:S(2)}, u32[]{:S(2)}) collective-permute-start(bf16[4,288,256]{2,1,0:T(8,128)(2,1)} %get-tuple-element.127), channel_id=1, source_target_pairs={{0,2},{2,4},{4,6},{6,0},{1,3},{3,5},{5,7},{7,1},{8,10},{10,12},{12... | collective-permute-start | bytes 1769480 | tf_op jit(solution)/shard_map/ppermute | solution.py:367
  370.0 34.6 %collective-permute-start.18 = (bf16[4,288,256]{2,1,0:T(8,128)(2,1)}, bf16[4,288,256]{2,1,0:T(8,128)(2,1)S(1)}, u32[]{:S(2)}, u32[]{:S(2)}) collective-permute-start(bf16[4,288,256]{2,1,0:T(8,128)(2,1)} %get-tuple-element.126), channel_id=1, source_target_pairs={{0,4},{2,6},{4,0},{6,2},{1,5},{3,7},{5,1},{7,3},{8,12},{10,14},{12... | collective-permute-start | bytes 1769480 | tf_op jit(solution)/shard_map/ppermute | solution.py:367
  378.8 27.6 %collective-permute-start.19 = (bf16[4,288,256]{2,1,0:T(8,128)(2,1)}, bf16[4,288,256]{2,1,0:T(8,128)(2,1)S(1)}, u32[]{:S(2)}, u32[]{:S(2)}) collective-permute-start(bf16[4,288,256]{2,1,0:T(8,128)(2,1)} %get-tuple-element.125), channel_id=1, source_target_pairs={{0,6},{2,0},{4,2},{6,4},{1,7},{3,1},{5,3},{7,5},{8,14},{10,8},{12,... | collective-permute-start | bytes 1769480 | tf_op jit(solution)/shard_map/ppermute | solution.py:367
  393.2 13.2 %copy-start.3 = (bf16[4,2,288,256]{3,2,1,0:T(8,128)(2,1)}, bf16[4,2,288,256]{3,2,1,0:T(8,128)(2,1)S(1)}, u32[]{:S(2)}) copy-start(bf16[4,2,288,256]{3,2,1,0:T(8,128)(2,1)S(1)} %collective-permute-done.23.refs_17_) | copy-start | bytes 3538948
  393.2 13.2 %copy-start.6 = (bf16[4,288,256]{2,1,0:T(8,128)(2,1)}, bf16[4,288,256]{2,1,0:T(8,128)(2,1)S(1)}, u32[]{:S(2)}) copy-start(bf16[4,288,256]{2,1,0:T(8,128)(2,1)S(1)} %collective-permute-done.17.refs_13_) | copy-start | bytes 1769476
  404.5 1.9 copy-start.7
  406.4 0.9 copy-start.8
  468.8 5.2 %copy-start.10 = (f32[64,256]{1,0:T(8,128)S(1)}, f32[64,256]{1,0:T(8,128)}, u32[]{:S(2)}) copy-start(f32[64,256]{1,0:T(8,128)} %get-tuple-element.116) | copy-start | bytes 196612
  468.8 5.8 %copy-start.5 = (f32[64,896]{1,0:T(8,128)S(1)}, f32[64,896]{1,0:T(8,128)}, u32[]{:S(2)}) copy-start(f32[64,896]{1,0:T(8,128)} %convert_add_fusion.2) | copy-start | bytes 688132
  472.0 4.4 copy-start
  476.4 8.9 %copy-start.9 = (f32[64,512]{1,0:T(8,128)S(1)}, f32[64,512]{1,0:T(8,128)}, u32[]{:S(2)}) copy-start(f32[64,512]{1,0:T(8,128)} %get-tuple-element.162) | copy-start | bytes 393220
Sparse Core Ops, SparseCore 0:
  257.0 109.9 reduce-scatter.1
where the time goes:
time: 502 us; the launch traced here: 493 us
  Pallas kernels  318 us (63%)
  starting transfers between devices  91.6 us (18%)
  waiting for transfers between devices  37.1 us (7%)
  other arithmetic  17.6 us (4%)
  between operations  14.7 us (3%)
  local copies, waits for them, and re-layouts  14.5 us (3%)
    pallas_call x1, Pallas kernels, feed(): pl.pallas_call(feed_kernel, grid=(count,), in_specs=[seq, seq, row, colum...  87.8 us
    ppermute x12, starting transfers between devices, shift(): lax.ppermute(value, axis, [(i, (i + by) % size) for i in range(size)])  73.2 us
    pallas_call x1, Pallas kernels, early_grads(): pl.pallas_call(functools.partial(early_kernel, split, cut), grid=(2 * til...  64.4 us
    pallas_call x1, Pallas kernels, tail(): pl.pallas_call(kernel, grid=(count,), in_specs=[seq, pl.BlockSpec((own, d...  61.5 us
    pallas_call x3, Pallas kernels, attend_backward(): pl.pallas_call(functools.partial(attend_back_kernel, groups, heads, first...  43.9 us
    pallas_call x1, Pallas kernels, project(): pl.pallas_call(functools.partial(project_kernel, sent), grid=(count,), in...  39.8 us
    ppermute x12, waiting for transfers between devices, shift(): lax.ppermute(value, axis, [(i, (i + by) % size) for i in range(size)])  35.5 us
    pallas_call x3, Pallas kernels, attend_forward(): pl.pallas_call(functools.partial(attend_kernel, groups, heads, first, inp...  20.3 us
  transfers between devices with their start and end apart: 25, of which 6 were waited for; matrix products, arithmetic and copies ran while one was open for 2% of the time, Pallas kernels for 13%

commit v1 on v0

--- a/solution.py
+++ b/solution.py
@@ -1396,6 +1396,7 @@
 
     @pl.when(step == 0)
     def _():
+        start(loads)
         barrier = pltpu.get_barrier_semaphore()
         for peer in peers:
             pl.semaphore_signal(barrier, inc=1, device_id=peer, device_id_type=pl.DeviceIdType.MESH)
@@ -1404,14 +1405,13 @@
         join(keep_mid, got_mid, sum_mid)
         start(key_copies[0])
         start(early_copies)
-        start(loads)
-        end_core.wait()
-        join(keep_end, got_end, sum_end)
-        start(key_copies[1])
         for load in loads:
             load.wait()
         query_stage[...] = query_product(1 - core).astype(BF)
         start([query_core])
+        end_core.wait()
+        join(keep_end, got_end, sum_end)
+        start(key_copies[1])
         dw[...] = jnp.zeros(dw.shape, F32)
         gg1[...] = jnp.zeros(gg1.shape, F32)
 

time: 502 us -> 502 us (level)
  transfers between devices with their start and end apart: 25 -> 25, of which waited for: 6 -> 7; matrix products, arithmetic and copies ran while one was open for 2% -> 2% of each run, Pallas kernels for 13% -> 13%
where the time goes in v1:
time: 502 us; the launch traced here: 496 us
  Pallas kernels  319 us (64%)
  starting transfers between devices  92.2 us (18%)
  waiting for transfers between devices  37.1 us (7%)
  other arithmetic  17.6 us (4%)
  local copies, waits for them, and re-layouts  14.7 us (3%)
  between operations  14.7 us (3%)
    pallas_call x1, Pallas kernels, feed(): pl.pallas_call(feed_kernel, grid=(count,), in_specs=[seq, seq, row, colum...  87.8 us
    ppermute x12, starting transfers between devices, shift(): lax.ppermute(value, axis, [(i, (i + by) % size) for i in range(size)])  73.7 us
    pallas_call x1, Pallas kernels, early_grads(): pl.pallas_call(functools.partial(early_kernel, split, cut), grid=(2 * til...  64.4 us
    pallas_call x1, Pallas kernels, tail(): pl.pallas_call(kernel, grid=(count,), in_specs=[seq, pl.BlockSpec((own, d...  63.1 us
    pallas_call x3, Pallas kernels, attend_backward(): pl.pallas_call(functools.partial(attend_back_kernel, groups, heads, first...  44.1 us
    pallas_call x1, Pallas kernels, project(): pl.pallas_call(functools.partial(project_kernel, sent), grid=(count,), in...  39.8 us
    ppermute x12, waiting for transfers between devices, shift(): lax.ppermute(value, axis, [(i, (i + by) % size) for i in range(size)])  35.5 us
    pallas_call x3, Pallas kernels, attend_forward(): pl.pallas_call(functools.partial(attend_kernel, groups, heads, first, inp...  20.3 us
  transfers between devices with their start and end apart: 25, of which 7 were waited for; matrix products, arithmetic and copies ran while one was open for 2% of the time, Pallas kernels for 13%

profile of v1, /device:TPU:0, one launch (start us, length us, event | category | flops | bytes accessed | tf_op | source)
XLA Modules:
  0.0 495.6 jit_solution(13423107016995884943)
XLA Ops:
  7.2 0.5 collective-permute-start.2
  7.8 0.4 collective-permute-start.1
  8.3 1.3 broadcast_in_dim.60
  9.6 1.7 copy.31.wr_ref
  11.2 1.3 broadcast_in_dim.61
  12.5 0.8 multiply_sine_fusion.1
  13.3 1.5 collective-permute-done.1.wtp_ref
  14.8 0.6 copy-done.18
  15.4 0.9 copy-done.17
  16.4 39.8 %project.1 = (bf16[4,288,256]{2,1,0:T(8,128)(2,1)}, bf16[8,1024,256]{2,1,0:T(8,128)(2,1)}, bf16[8,1024,256]{2,1,0:T(8,128)(2,1)}, bf16[2048,2816]{1,0:T(8,128)(2...) custom-call(bf16[8,256,1024]{2,1,0:T(8,128)(2,1)} %refs_0_.1, ...), custom_call_target="tpu_custom_call" | custom-call | flops 30000001024 | tf_op jit(solution)/shard_map/project/pallas_call | solution.py:534
  56.2 2.4 collective-permute-start.5
  58.6 0.6 collective-permute-start.4
  59.1 0.5 collective-permute-start.3
  59.7 7.2 %attend.3 = (bf16[8,1024,256]{2,1,0:T(8,128)(2,1)}, f32[8,4,1024]{2,1,0:T(4,128)}) custom-call(s32[8,8]{1,0:T(8,128)} %docs_ref.11, bf16[8,1024,256]{2,1,0:T(8,128)(2,1)} %get-tuple-element.101.q_ref, bf16[4,4,288,256]{3,2,1,0:T(8,128)(2,1)} %get-tuple-element.68.refs_0_, bf16[4,4,288,256]{3,2,1,0:T(8,128)(2,1)} %get-tuple-element.69.refs_1_), custom_call_target="tpu_custom_call" | custom-call | flops 30000001024 | tf_op jit(solution)/shard_map/attend/pallas_call | solution.py:758
  66.8 4.1 collective-permute-start.6
  71.0 1.7 collective-permute-done.5
  72.7 14.1 %collective-permute-done.4 = bf16[4,288,256]{2,1,0:T(8,128)(2,1)} collective-permute-done((bf16[4,288,256]{2,1,0:T(8,128)(2,1)}, bf16[4,288,256]{2,1,0:T(8,128)(2,1)}, u32[]{:S(2)}, u32[]{:S(2)}) %collective-permute-start.4) | collective-permute-done | bytes 589856 | tf_op jit(solution)/shard_map/ppermute | solution.py:367
  86.8 0.5 collective-permute-start.8
  87.3 4.3 attend.4
  91.7 2.3 collective-permute-start.11
  94.0 8.9 %attend.5 = (bf16[8,1024,256]{2,1,0:T(8,128)(2,1)}, f32[8,4,1024]{2,1,0:T(4,128)}) custom-call(s32[8,8]{1,0:T(8,128)} %docs_ref.11, bf16[8,1024,256]{2,1,0:T(8,128)(2,1)} %get-tuple-element.101.q_ref, bf16[1,4,288,256]{3,2,1,0:T(8,128)(2,1)} %bitcast.1.refs_0_, ...), custom_call_target="tpu_custom_call", output_to_operand_aliasing={{0}: (10, {}), {1}: (11, {})} | custom-call | flops 40000000000 | tf_op jit(solution)/shard_map/attend/pallas_call | solution.py:758
  102.9 0.1 broadcast_select_fusion.1
  103.1 1.6 pad_maximum_fusion.wo_ref
  104.6 87.8 %feed.1 = (bf16[8,256,1024]{2,1,0:T(8,128)(2,1)}, bf16[8,1024,256]{2,1,0:T(8,128)(2,1)}, bf16[8,1024,256]{2,1,0:T(8,128)(2,1)}, bf16[22,2048,128]{2,1,0:T(8,128)...) custom-call(bf16[8,256,1024]{2,1,0:T(8,128)(2,1)} %refs_0_.1, ...), custom_call_target="tpu_custom_call" | custom-call | flops 67645734912 | tf_op jit(solution)/shard_map/feed/pallas_call | solution.py:1086
  192.4 64.4 %early_grads.1 = (bf16[1024,3840]{1,0:T(8,128)(2,1)}, bf16[1024,896]{1,0:T(8,128)(2,1)}) custom-call(bf16[8,1024,256]{2,1,0:T(8,128)(2,1)} %get-tuple-element.86.nt_ref, bf16[22,2048,128]{2,1,0:T(8,128)(2,1)} %get-tuple-element.87.gg_ref, bf16[22,2048,128]{2,1,0:T(8,128)(2,1)} %get-tuple-element.88.gu_ref, ...), custom_call_target="tpu_custom_call" | custom-call | flops 60000002048 | tf_op jit(solution)/shard_map/early_grads/pallas_call | solution.py:1260
  256.9 0.6 copy-done.12
  257.5 0.5 multiply_cosine_fusion
  258.0 0.2 concatenate.23
  258.3 0.2 concatenate.24
  258.6 0.2 concatenate.22
  259.0 0.2 collective-permute-start.13
  259.2 2.6 collective-permute-start.14
  261.8 2.7 collective-permute-start.15
  264.6 0.8 maximum_multiply_fusion.rot_ref
  265.4 20.5 %attend_back.3 = (bf16[2048,1024]{1,0:T(8,128)(2,1)}, bf16[4,4,288,256]{3,2,1,0:T(8,128)(2,1)}, bf16[4,4,288,256]{3,2,1,0:T(8,128)(2,1)}) custom-call(s32[8,8]{1,0:T(8,128)} %docs_ref.11, bf16[8,1024,256]{2,1,0:T(8,128)(2,1)} %get-tuple-element.101.q_ref, bf16[8,1024,256]{2,1,0:T(8,128)(2,1)} %get-tuple-element.95.do_ref, ...), custom_call_target="tpu_custom_call" | custom-call | flops 4000000000 | tf_op jit(solution)/shard_map/attend_back/pallas_call | solution.py:941
  285.9 6.5 %collective-permute-done.14 = bf16[4,64,896]{2,1,0:T(8,128)(2,1)S(1)} collective-permute-done((bf16[4,64,896]{2,1,0:T(8,128)(2,1)S(1)}, bf16[4,64,896]{2,1,0:T(8,128)(2,1)S(1)}, u32[]{:S(2)}, u32[]{:S(2)}) %collective-permute-start.14) | collective-permute-done | bytes 458784 | tf_op jit(solution)/shard_map/ppermute | solution.py:367
  292.4 0.2 fusion.2
  292.6 5.9 %collective-permute-start.16 = (bf16[4,4,288,256]{3,2,1,0:T(8,128)(2,1)}, bf16[4,4,288,256]{3,2,1,0:T(8,128)(2,1)S(1)}, u32[]{:S(2)}, u32[]{:S(2)}) collective-permute-start(bf16[4,4,288,256]{3,2,1,0:T(8,128)(2,1)} %get-tuple-element.100), channel_id=1, source_target_pairs={{0,1},{1,0},{2,3},{3,2},{4,5},{5,4},{6,7},{7,6},{8,9},{9,8},{10,11... | collective-permute-start | bytes 7077896 | tf_op jit(solution)/shard_map/ppermute | solution.py:362
  298.6 19.7 %collective-permute-start.20 = (bf16[64,896]{1,0:T(8,128)(2,1)S(1)}, bf16[64,896]{1,0:T(8,128)(2,1)S(1)}, u32[]{:S(2)}, u32[]{:S(2)}) collective-permute-start(bf16[64,896]{1,0:T(8,128)(2,1)S(1)} %get-tuple-element.136), channel_id=1, source_target_pairs={{0,2},{2,4},{4,6},{6,0},{1,3},{3,5},{5,7},{7,1},{8,10},{10,12},{12... | collective-permute-start | bytes 344072 | tf_op jit(solution)/shard_map/ppermute | solution.py:367
  318.3 30.7 %collective-permute-start.21 = (bf16[64,896]{1,0:T(8,128)(2,1)S(1)}, bf16[64,896]{1,0:T(8,128)(2,1)S(1)}, u32[]{:S(2)}, u32[]{:S(2)}) collective-permute-start(bf16[64,896]{1,0:T(8,128)(2,1)S(1)} %get-tuple-element.138), channel_id=1, source_target_pairs={{0,4},{2,6},{4,0},{6,2},{1,5},{3,7},{5,1},{7,3},{8,12},{10,14},{12... | collective-permute-start | bytes 344072 | tf_op jit(solution)/shard_map/ppermute | solution.py:367
  349.0 12.2 %attend_back.4 = (bf16[2048,1024]{1,0:T(8,128)(2,1)}, bf16[4,2,288,256]{3,2,1,0:T(8,128)(2,1)}, bf16[4,2,288,256]{3,2,1,0:T(8,128)(2,1)}) custom-call(s32[8,8]{1,0:T(8,128)} %docs_ref.11, bf16[8,1024,256]{2,1,0:T(8,128)(2,1)} %get-tuple-element.101.q_ref, bf16[8,1024,256]{2,1,0:T(8,128)(2,1)} %get-tuple-element.95.do_ref, ...), custom_call_target="tpu_custom_call", output_to_operand_aliasing={{0}: (8, {})} | custom-call | flops 2000000000 | tf_op jit(solution)/shard_map/attend_back/pallas_call | solution.py:941
  361.2 0.7 convert_add_fusion.2
  361.9 4.4 collective-permute-start.23
  366.3 1.9 fusion.6
  368.2 3.7 collective-permute-start.17
  371.9 8.9 %collective-permute-start.18 = (bf16[4,288,256]{2,1,0:T(8,128)(2,1)}, bf16[4,288,256]{2,1,0:T(8,128)(2,1)S(1)}, u32[]{:S(2)}, u32[]{:S(2)}) collective-permute-start(bf16[4,288,256]{2,1,0:T(8,128)(2,1)} %get-tuple-element.126), channel_id=1, source_target_pairs={{0,4},{2,6},{4,0},{6,2},{1,5},{3,7},{5,1},{7,3},{8,12},{10,14},{12... | collective-permute-start | bytes 1769480 | tf_op jit(solution)/shard_map/ppermute | solution.py:367
  380.7 1.7 collective-permute-start.19
  382.5 11.4 %attend_back.5 = (bf16[2048,1024]{1,0:T(8,128)(2,1)}, bf16[4,2,288,256]{3,2,1,0:T(8,128)(2,1)}, bf16[4,2,288,256]{3,2,1,0:T(8,128)(2,1)}) custom-call(s32[8,8]{1,0:T(8,128)} %docs_ref.11, bf16[8,1024,256]{2,1,0:T(8,128)(2,1)} %get-tuple-element.101.q_ref, bf16[8,1024,256]{2,1,0:T(8,128)(2,1)} %get-tuple-element.95.do_ref, ...), custom_call_target="tpu_custom_call", output_to_operand_aliasing={{0}: (8, {})} | custom-call | flops 2000000000 | tf_op jit(solution)/shard_map/attend_back/pallas_call | solution.py:941
  393.9 0.7 collective-permute-done.17.refs_13_
  394.6 12.4 %collective-permute-done.18.refs_14_ = bf16[4,288,256]{2,1,0:T(8,128)(2,1)S(1)} collective-permute-done((bf16[4,288,256]{2,1,0:T(8,128)(2,1)}, bf16[4,288,256]{2,1,0:T(8,128)(2,1)S(1)}, u32[]{:S(2)}, u32[]{:S(2)}) %collective-permute-start.18) | collective-permute-done | bytes 589856 | tf_op jit(solution)/shard_map/ppermute | solution.py:367
  407.1 0.7 copy-done.7
  407.9 0.2 copy-done.8
  408.1 63.1 %tail.1 = (bf16[8,256,1024]{2,1,0:T(8,128)(2,1)}, f32[64,512]{1,0:T(8,128)}, f32[64,256]{1,0:T(8,128)}, f32[64,3840]{1,0:T(8,128)}) custom-call(bf16[8,256,1024]{2,1,0:T(8,128)(2,1)} %refs_0_.1, bf16[2048,1024]{1,0:T(8,128)(2,1)} %get-tuple-element.104.refs_1_.refs_10_, bf16[8,1024,256]{2,1,0:T(8,128)(2,1)} %get-tuple-element.105.refs_2_.refs_9_, ...), custom_call_target="tpu_custom_call" | custom-call | flops 100000000 | tf_op jit(solution)/shard_map/tail/pallas_call | solution.py:1547
  471.3 1.7 fusion.8
  473.0 1.2 slice.68
  474.1 0.4 reshape.62
  474.5 1.9 slice_reduce_fusion
  476.5 0.6 fusion.9
  477.1 0.8 maximum_bitcast_fusion
  477.8 1.1 copy_bitcast_fusion
  478.9 7.6 %convert_add_fusion = f32[8,256,1024]{2,1,0:T(8,128)} fusion(bf16[8,256,1024]{2,1,0:T(8,128)(2,1)} %get-tuple-element.115, bf16[8,256,1024]{2,1,0:T(8,128)(2,1)S(1)} %copy-done), kind=kLoop, calls=%fused_computation | loop fusion | flops 6291456 | bytes 16777216 | tf_op jit(solution)/shard_map/add | solution.py:1692
  486.5 0.6 constant_dynamic-slice_fusion
  487.1 0.7 dynamic-slice_reduce_fusion
  487.8 0.7 copy.44
  (67 shorter events, 0.8 us)
Async XLA Ops:
  7.2 399.9 %reduce-scatter.2.cloned.1.call-start = ((), (), s32[]{:S(2)}) async-start(), calls=%async_computation.1 | async-start | bytes 9830400 | tf_op jit(solution)/shard_map/reduce_scatter | solution.py:1657
  7.2 7.6 %collective-permute-start.2 = (bf16[1408,1024]{1,0:T(8,128)(2,1)}, bf16[1408,1024]{1,0:T(8,128)(2,1)S(1)}, u32[]{:S(2)}, u32[]{:S(2)}) collective-permute-start(bf16[1408,1024]{1,0:T(8,128)(2,1)} %wdo_ref.3), channel_id=1, source_target_pairs={{0,1},{1,0},{2,3},{3,2},{4,5},{5,4},{6,7},{7,6},{8,9},{9,8},{10,11... | collective-permute-start | bytes 8650760 | tf_op jit(solution)/shard_map/ppermute | solution.py:362
  7.7 7.0 %collective-permute-start = (bf16[1024,512]{1,0:T(8,128)(2,1)}, bf16[1024,512]{1,0:T(8,128)(2,1)}, u32[]{:S(2)}, u32[]{:S(2)}) collective-permute-start(bf16[1024,512]{1,0:T(8,128)(2,1)} %wqo_ref.1), channel_id=1, source_target_pairs={{0,1},{1,0},{2,3},{3,2},{4,5},{5,4},{6,7},{7,6},{8,9},{9,8},{10,11... | collective-permute-start | bytes 3145736 | tf_op jit(solution)/shard_map/ppermute | solution.py:362
  7.8 6.9 %collective-permute-start.1 = (bf16[1024,128]{1,0:T(8,128)(2,1)}, bf16[1024,128]{1,0:T(8,128)(2,1)S(1)}, u32[]{:S(2)}, u32[]{:S(2)}) collective-permute-start(bf16[1024,128]{1,0:T(8,128)(2,1)} %wto_ref.1), channel_id=1, source_target_pairs={{0,1},{1,0},{2,3},{3,2},{4,5},{5,4},{6,7},{7,6},{8,9},{9,8},{10,11... | collective-permute-start | bytes 786440 | tf_op jit(solution)/shard_map/ppermute | solution.py:362
  8.3 47.9 %copy-start.11 = (f32[256]{0:T(256)}, f32[256]{0:T(256)S(1)}, u32[]{:S(2)}) copy-start(f32[256]{0:T(256)S(1)} %add_convert_fusion.4) | copy-start | bytes 3076
  8.3 47.9 %copy-start.13 = (f32[16]{0:T(128)}, f32[16]{0:T(128)S(1)}, u32[]{:S(2)}) copy-start(f32[16]{0:T(128)S(1)} %multiply_power_fusion) | copy-start | bytes 196
  14.7 0.7 copy-start.18
  14.8 1.6 copy-start.17
  56.2 16.5 %collective-permute-start.5 = (bf16[4,288,256]{2,1,0:T(8,128)(2,1)}, bf16[4,288,256]{2,1,0:T(8,128)(2,1)}, u32[]{:S(2)}, u32[]{:S(2)}) collective-permute-start(bf16[4,288,256]{2,1,0:T(8,128)(2,1)} %get-tuple-element.72), channel_id=1, source_target_pairs={{0,6},{2,0},{4,2},{6,4},{1,7},{3,1},{5,3},{7,5},{8,14},{10,8},{12,... | collective-permute-start | bytes 1769480 | tf_op jit(solution)/shard_map/ppermute | solution.py:367
  58.6 28.3 %collective-permute-start.4 = (bf16[4,288,256]{2,1,0:T(8,128)(2,1)}, bf16[4,288,256]{2,1,0:T(8,128)(2,1)}, u32[]{:S(2)}, u32[]{:S(2)}) collective-permute-start(bf16[4,288,256]{2,1,0:T(8,128)(2,1)} %get-tuple-element.72), channel_id=1, source_target_pairs={{0,4},{2,6},{4,0},{6,2},{1,5},{3,7},{5,1},{7,3},{8,12},{10,14},{12... | collective-permute-start | bytes 1769480 | tf_op jit(solution)/shard_map/ppermute | solution.py:367
  59.1 27.7 %collective-permute-start.3 = (bf16[4,288,256]{2,1,0:T(8,128)(2,1)}, bf16[4,288,256]{2,1,0:T(8,128)(2,1)}, u32[]{:S(2)}, u32[]{:S(2)}) collective-permute-start(bf16[4,288,256]{2,1,0:T(8,128)(2,1)} %get-tuple-element.72), channel_id=1, source_target_pairs={{0,2},{2,4},{4,6},{6,0},{1,3},{3,5},{5,7},{7,1},{8,10},{10,12},{12... | collective-permute-start | bytes 1769480 | tf_op jit(solution)/shard_map/ppermute | solution.py:367
  59.7 11.2 %copy-start.4 = (bf16[512,1024]{1,0:T(8,128)(2,1)S(1)}, bf16[512,1024]{1,0:T(8,128)(2,1)}, u32[]{:S(2)}) copy-start(bf16[512,1024]{1,0:T(8,128)(2,1)} %param.17) | copy-start | bytes 3145732
  66.8 24.8 %copy-start.15 = (bf16[1024,1408]{1,0:T(8,128)(2,1)S(1)}, bf16[1024,1408]{1,0:T(8,128)(2,1)}, u32[]{:S(2)}) copy-start(bf16[1024,1408]{1,0:T(8,128)(2,1)} %wgo_ref.1) | copy-start | bytes 8650756
  66.8 27.1 %copy-start.16 = (bf16[1024,1408]{1,0:T(8,128)(2,1)S(1)}, bf16[1024,1408]{1,0:T(8,128)(2,1)}, u32[]{:S(2)}) copy-start(bf16[1024,1408]{1,0:T(8,128)(2,1)} %wuo_ref.1) | copy-start | bytes 8650756
  66.8 24.8 %collective-permute-start.6 = (bf16[4,288,256]{2,1,0:T(8,128)(2,1)}, bf16[4,288,256]{2,1,0:T(8,128)(2,1)}, u32[]{:S(2)}, u32[]{:S(2)}) collective-permute-start(bf16[4,288,256]{2,1,0:T(8,128)(2,1)} %get-tuple-element.72), channel_id=1, source_target_pairs={{0,1},{1,0},{2,3},{3,2},{4,5},{5,4},{6,7},{7,6},{8,9},{9,8},{10,11... | collective-permute-start | bytes 1769480 | tf_op jit(solution)/shard_map/ppermute | solution.py:362
  70.9 32.0 %collective-permute-start.10 = (bf16[512,1024]{1,0:T(8,128)(2,1)S(1)}, bf16[512,1024]{1,0:T(8,128)(2,1)S(1)}, u32[]{:S(2)}, u32[]{:S(2)}) collective-permute-start(bf16[512,1024]{1,0:T(8,128)(2,1)S(1)} %copy-done.4), channel_id=1, source_target_pairs={{0,1},{1,0},{2,3},{3,2},{4,5},{5,4},{6,7},{7,6},{8,9},{9,8},{10,11... | collective-permute-start | bytes 3145736 | tf_op jit(solution)/shard_map/ppermute | solution.py:362
  86.8 7.1 %collective-permute-start.9 = (bf16[4,288,256]{2,1,0:T(8,128)(2,1)}, bf16[4,288,256]{2,1,0:T(8,128)(2,1)}, u32[]{:S(2)}, u32[]{:S(2)}) collective-permute-start(bf16[4,288,256]{2,1,0:T(8,128)(2,1)} %collective-permute-done.5), channel_id=1, source_target_pairs={{0,1},{1,0},{2,3},{3,2},{4,5},{5,4},{6,7},{7,6},{8,9},{9,8},{10,11... | collective-permute-start | bytes 1769480 | tf_op jit(solution)/shard_map/ppermute | solution.py:362
  86.8 7.2 %collective-permute-start.8 = (bf16[4,288,256]{2,1,0:T(8,128)(2,1)}, bf16[4,288,256]{2,1,0:T(8,128)(2,1)}, u32[]{:S(2)}, u32[]{:S(2)}) collective-permute-start(bf16[4,288,256]{2,1,0:T(8,128)(2,1)} %collective-permute-done.4), channel_id=1, source_target_pairs={{0,1},{1,0},{2,3},{3,2},{4,5},{5,4},{6,7},{7,6},{8,9},{9,8},{10,11... | collective-permute-start | bytes 1769480 | tf_op jit(solution)/shard_map/ppermute | solution.py:362
  87.3 6.7 %collective-permute-start.7 = (bf16[4,288,256]{2,1,0:T(8,128)(2,1)}, bf16[4,288,256]{2,1,0:T(8,128)(2,1)}, u32[]{:S(2)}, u32[]{:S(2)}) collective-permute-start(bf16[4,288,256]{2,1,0:T(8,128)(2,1)} %collective-permute-done.3), channel_id=1, source_target_pairs={{0,1},{1,0},{2,3},{3,2},{4,5},{5,4},{6,7},{7,6},{8,9},{9,8},{10,11... | collective-permute-start | bytes 1769480 | tf_op jit(solution)/shard_map/ppermute | solution.py:362
  91.7 13.0 %collective-permute-start.11 = (bf16[1024,1408]{1,0:T(8,128)(2,1)S(1)}, bf16[1024,1408]{1,0:T(8,128)(2,1)}, u32[]{:S(2)}, u32[]{:S(2)}) collective-permute-start(bf16[1024,1408]{1,0:T(8,128)(2,1)S(1)} %copy-done.15), channel_id=1, source_target_pairs={{0,1},{1,0},{2,3},{3,2},{4,5},{5,4},{6,7},{7,6},{8,9},{9,8},{10,11... | collective-permute-start | bytes 8650760 | tf_op jit(solution)/shard_map/ppermute | solution.py:362
  93.9 10.7 %collective-permute-start.12 = (bf16[1024,1408]{1,0:T(8,128)(2,1)S(1)}, bf16[1024,1408]{1,0:T(8,128)(2,1)}, u32[]{:S(2)}, u32[]{:S(2)}) collective-permute-start(bf16[1024,1408]{1,0:T(8,128)(2,1)S(1)} %copy-done.16), channel_id=1, source_target_pairs={{0,1},{1,0},{2,3},{3,2},{4,5},{5,4},{6,7},{7,6},{8,9},{9,8},{10,11... | collective-permute-start | bytes 8650760 | tf_op jit(solution)/shard_map/ppermute | solution.py:362
  256.8 0.7 copy-start.12
  256.8 0.7 copy-start.14
  256.8 2.0 copy-start.2
  259.0 26.9 %collective-permute-start.13 = (bf16[4,64,896]{2,1,0:T(8,128)(2,1)S(1)}, bf16[4,64,896]{2,1,0:T(8,128)(2,1)S(1)}, u32[]{:S(2)}, u32[]{:S(2)}) collective-permute-start(bf16[4,64,896]{2,1,0:T(8,128)(2,1)S(1)} %get-tuple-element.131), channel_id=1, source_target_pairs={{0,8},{8,16},{16,24},{24,0},{1,9},{9,17},{17,25},{25,1},{2,10},{10... | collective-permute-start | bytes 1376264 | tf_op jit(solution)/shard_map/ppermute | solution.py:367
  259.2 33.1 %collective-permute-start.14 = (bf16[4,64,896]{2,1,0:T(8,128)(2,1)S(1)}, bf16[4,64,896]{2,1,0:T(8,128)(2,1)S(1)}, u32[]{:S(2)}, u32[]{:S(2)}) collective-permute-start(bf16[4,64,896]{2,1,0:T(8,128)(2,1)S(1)} %get-tuple-element.133), channel_id=1, source_target_pairs={{0,16},{8,24},{16,0},{24,8},{1,17},{9,25},{17,1},{25,9},{2,18},{10... | collective-permute-start | bytes 1376264 | tf_op jit(solution)/shard_map/ppermute | solution.py:367
  261.8 30.5 %collective-permute-start.15 = (bf16[4,64,896]{2,1,0:T(8,128)(2,1)S(1)}, bf16[4,64,896]{2,1,0:T(8,128)(2,1)S(1)}, u32[]{:S(2)}, u32[]{:S(2)}) collective-permute-start(bf16[4,64,896]{2,1,0:T(8,128)(2,1)S(1)} %get-tuple-element.132), channel_id=1, source_target_pairs={{0,24},{8,0},{16,8},{24,16},{1,25},{9,1},{17,9},{25,17},{2,26},{10... | collective-permute-start | bytes 1376264 | tf_op jit(solution)/shard_map/ppermute | solution.py:367
  292.6 73.7 %collective-permute-start.16 = (bf16[4,4,288,256]{3,2,1,0:T(8,128)(2,1)}, bf16[4,4,288,256]{3,2,1,0:T(8,128)(2,1)S(1)}, u32[]{:S(2)}, u32[]{:S(2)}) collective-permute-start(bf16[4,4,288,256]{3,2,1,0:T(8,128)(2,1)} %get-tuple-element.100), channel_id=1, source_target_pairs={{0,1},{1,0},{2,3},{3,2},{4,5},{5,4},{6,7},{7,6},{8,9},{9,8},{10,11... | collective-permute-start | bytes 7077896 | tf_op jit(solution)/shard_map/ppermute | solution.py:362
  298.6 62.6 %collective-permute-start.20 = (bf16[64,896]{1,0:T(8,128)(2,1)S(1)}, bf16[64,896]{1,0:T(8,128)(2,1)S(1)}, u32[]{:S(2)}, u32[]{:S(2)}) collective-permute-start(bf16[64,896]{1,0:T(8,128)(2,1)S(1)} %get-tuple-element.136), channel_id=1, source_target_pairs={{0,2},{2,4},{4,6},{6,0},{1,3},{3,5},{5,7},{7,1},{8,10},{10,12},{12... | collective-permute-start | bytes 344072 | tf_op jit(solution)/shard_map/ppermute | solution.py:367
  318.3 42.9 %collective-permute-start.21 = (bf16[64,896]{1,0:T(8,128)(2,1)S(1)}, bf16[64,896]{1,0:T(8,128)(2,1)S(1)}, u32[]{:S(2)}, u32[]{:S(2)}) collective-permute-start(bf16[64,896]{1,0:T(8,128)(2,1)S(1)} %get-tuple-element.138), channel_id=1, source_target_pairs={{0,4},{2,6},{4,0},{6,2},{1,5},{3,7},{5,1},{7,3},{8,12},{10,14},{12... | collective-permute-start | bytes 344072 | tf_op jit(solution)/shard_map/ppermute | solution.py:367
  349.0 12.2 %collective-permute-start.22 = (bf16[64,896]{1,0:T(8,128)(2,1)S(1)}, bf16[64,896]{1,0:T(8,128)(2,1)S(1)}, u32[]{:S(2)}, u32[]{:S(2)}) collective-permute-start(bf16[64,896]{1,0:T(8,128)(2,1)S(1)} %get-tuple-element.137), channel_id=1, source_target_pairs={{0,6},{2,0},{4,2},{6,4},{1,7},{3,1},{5,3},{7,5},{8,14},{10,8},{12,... | collective-permute-start | bytes 344072 | tf_op jit(solution)/shard_map/ppermute | solution.py:367
  349.0 17.3 %copy-start.1 = (bf16[4,4,288,256]{3,2,1,0:T(8,128)(2,1)S(1)}, bf16[4,4,288,256]{3,2,1,0:T(8,128)(2,1)}, u32[]{:S(2)}) copy-start(bf16[4,4,288,256]{3,2,1,0:T(8,128)(2,1)} %get-tuple-element.97) | copy-start | bytes 7077892
  361.9 32.0 %collective-permute-start.23 = (bf16[4,2,288,256]{3,2,1,0:T(8,128)(2,1)}, bf16[4,2,288,256]{3,2,1,0:T(8,128)(2,1)S(1)}, u32[]{:S(2)}, u32[]{:S(2)}) collective-permute-start(bf16[4,2,288,256]{3,2,1,0:T(8,128)(2,1)} %get-tuple-element.112), channel_id=1, source_target_pairs={{0,1},{1,0},{2,3},{3,2},{4,5},{5,4},{6,7},{7,6},{8,9},{9,8},{10,11... | collective-permute-start | bytes 3538952 | tf_op jit(solution)/shard_map/ppermute | solution.py:362
  368.2 26.4 %collective-permute-start.17 = (bf16[4,288,256]{2,1,0:T(8,128)(2,1)}, bf16[4,288,256]{2,1,0:T(8,128)(2,1)S(1)}, u32[]{:S(2)}, u32[]{:S(2)}) collective-permute-start(bf16[4,288,256]{2,1,0:T(8,128)(2,1)} %get-tuple-element.127), channel_id=1, source_target_pairs={{0,2},{2,4},{4,6},{6,0},{1,3},{3,5},{5,7},{7,1},{8,10},{10,12},{12... | collective-permute-start | bytes 1769480 | tf_op jit(solution)/shard_map/ppermute | solution.py:367
  371.9 35.1 %collective-permute-start.18 = (bf16[4,288,256]{2,1,0:T(8,128)(2,1)}, bf16[4,288,256]{2,1,0:T(8,128)(2,1)S(1)}, u32[]{:S(2)}, u32[]{:S(2)}) collective-permute-start(bf16[4,288,256]{2,1,0:T(8,128)(2,1)} %get-tuple-element.126), channel_id=1, source_target_pairs={{0,4},{2,6},{4,0},{6,2},{1,5},{3,7},{5,1},{7,3},{8,12},{10,14},{12... | collective-permute-start | bytes 1769480 | tf_op jit(solution)/shard_map/ppermute | solution.py:367
  380.7 26.4 %collective-permute-start.19 = (bf16[4,288,256]{2,1,0:T(8,128)(2,1)}, bf16[4,288,256]{2,1,0:T(8,128)(2,1)S(1)}, u32[]{:S(2)}, u32[]{:S(2)}) collective-permute-start(bf16[4,288,256]{2,1,0:T(8,128)(2,1)} %get-tuple-element.125), channel_id=1, source_target_pairs={{0,6},{2,0},{4,2},{6,4},{1,7},{3,1},{5,3},{7,5},{8,14},{10,8},{12,... | collective-permute-start | bytes 1769480 | tf_op jit(solution)/shard_map/ppermute | solution.py:367
  393.9 13.2 %copy-start.3 = (bf16[4,2,288,256]{3,2,1,0:T(8,128)(2,1)}, bf16[4,2,288,256]{3,2,1,0:T(8,128)(2,1)S(1)}, u32[]{:S(2)}) copy-start(bf16[4,2,288,256]{3,2,1,0:T(8,128)(2,1)S(1)} %collective-permute-done.23.refs_17_) | copy-start | bytes 3538948
  394.6 12.5 %copy-start.6 = (bf16[4,288,256]{2,1,0:T(8,128)(2,1)}, bf16[4,288,256]{2,1,0:T(8,128)(2,1)S(1)}, u32[]{:S(2)}) copy-start(bf16[4,288,256]{2,1,0:T(8,128)(2,1)S(1)} %collective-permute-done.17.refs_13_) | copy-start | bytes 1769476
  407.0 0.8 copy-start.7
  407.1 1.0 copy-start.8
  471.2 5.2 %copy-start.10 = (f32[64,256]{1,0:T(8,128)S(1)}, f32[64,256]{1,0:T(8,128)}, u32[]{:S(2)}) copy-start(f32[64,256]{1,0:T(8,128)} %get-tuple-element.116) | copy-start | bytes 196612
  471.3 5.8 %copy-start.5 = (f32[64,896]{1,0:T(8,128)S(1)}, f32[64,896]{1,0:T(8,128)}, u32[]{:S(2)}) copy-start(f32[64,896]{1,0:T(8,128)} %convert_add_fusion.2) | copy-start | bytes 688132
  474.5 4.4 copy-start
  478.9 8.9 %copy-start.9 = (f32[64,512]{1,0:T(8,128)S(1)}, f32[64,512]{1,0:T(8,128)}, u32[]{:S(2)}) copy-start(f32[64,512]{1,0:T(8,128)} %get-tuple-element.162) | copy-start | bytes 393220
Sparse Core Ops, SparseCore 0:
  257.0 113.6 reduce-scatter.1
